TPU v7x, 256 devices: a whole 4x4x8 slice. The times are simulated.
256 devices in a mesh: wide: 32 (over z, x), narrow: 8 (over y, core).
Axes of the slice: x: 4, y: 4, z: 8, core: 2. Of those that a mesh axis runs over, the one named last changes fastest.
Arguments:
- initial: float32 [64, 512, 8192], P(None, 'wide', 'narrow'), may hold values from -50 to 50, as said below
- kappa: float32 [4, 512, 8192], P(None, 'wide', 'narrow'), may hold values from 0.3 to 1.2
- decay: float32 [512, 8192], P('wide', 'narrow'), may hold values from 0.05 to 0.5
- field_index: int32 [64], replicated, may hold values from 0 to 3
Outputs:
- basis: float32 [128, 512, 8192], P(None, 'wide', 'narrow')
- triangle: float32 [128, 128], replicated
Inputs may be any that keep to these rules, and one draw needn't show every extreme that they name: Every value of every sample's initial field lies in this range.
All inputs are finite; a program needn't handle non-finite values.
Results may differ from a plain program's by a relative error of at most 0.0003.
Values sent between devices are 32-bit elements; how exact they have to be, the bound alone decides.
No kernel may reach another device: no remote copies, remote signals or barrier semaphores. Data moves between devices by JAX's collectives and lax.ppermute only.
A program may use at most 128 MiB of HBM per device.

v0:
```python
import math

import jax
import jax.numpy as jnp
from jax import lax
from jax.sharding import PartitionSpec as P


def with_halo(shard, sides, width):
    for axis, dim in sides:
        count, length = (lax.axis_size(axis), shard.shape[dim])
        up = [(i, (i + 1) % count) for i in range(count - 1)]
        down = [(j, i) for i, j in up]
        last = lax.slice_in_dim(shard, length - width, length, axis=dim)
        leading = lax.slice_in_dim(shard, 0, width, axis=dim)
        before = lax.ppermute(last, axis, up)
        after = lax.ppermute(leading, axis, down)
        shard = jnp.concatenate([before, shard, after], axis=dim)
    return shard


def advance(padded, state, coefficient, decay):
    neighbours = (
        padded[:, 2:, 1:-1] + padded[:, :-2, 1:-1] + padded[:, 1:-1, 2:] + padded[:, 1:-1, :-2]
    )
    return state + 0.2 * coefficient * (neighbours - 4.0 * state) - decay * state


def select_fields(onehot, table):
    return jnp.einsum("sc,cxy->sxy", onehot, table, precision=lax.Precision.HIGHEST)


def gram_matrix(columns):
    return lax.dot_general(
        columns,
        columns,
        (((1,), (1,)), ((), ())),
        precision=lax.Precision.HIGHEST,
        preferred_element_type=jnp.float32,
    )


def shards(initial, kappa, decay, field_index):
    ncoef = kappa.shape[0]
    onehot = (field_index[:, None] == jnp.arange(ncoef, dtype=jnp.int32)[None, :]).astype(
        jnp.float32
    )
    coefficient = select_fields(onehot, kappa)
    padded = with_halo(initial, (("wide", 1), ("narrow", 2)), 1)
    first = advance(padded, initial, coefficient, decay)
    padded_next = with_halo(first, (("wide", 1), ("narrow", 2)), 1)
    second = advance(padded_next, first, coefficient, decay)
    snap_count = 2 * first.shape[0]
    snapshots = jnp.concatenate([first, second], 0).reshape(snap_count, -1)
    total = lax.psum(gram_matrix(snapshots), ("wide", "narrow"))
    lower_chol = jnp.linalg.cholesky(total)
    basis_rows = jax.scipy.linalg.solve_triangular(lower_chol, snapshots, lower=True)
    rfactor = lower_chol.T
    scale = math.sqrt(lax.axis_size("wide") * lax.axis_size("narrow") * snapshots.shape[1])
    basis = (basis_rows * scale).reshape(snap_count, first.shape[1], first.shape[2])
    return (basis, rfactor / scale)


def solution(mesh):
    placed = (P(None, "wide", "narrow"), P(None, "wide", "narrow"), P("wide", "narrow"), P())
    return jax.shard_map(
        shards,
        mesh=mesh,
        in_specs=placed,
        out_specs=(P(None, "wide", "narrow"), P()),
        check_vma=False,
    )
```

profile of v0, /device:TPU:1, one launch (start us, length us, event | category | flops | bytes accessed | tf_op | source)
XLA Modules:
  0.0 389.5 jit_solution(14842667507104307479)
XLA Ops:
  7.2 0.0 copy-start
  7.2 0.0 all-reduce.2.cloned.1.call-start
  7.2 4.8 %copy.42 = f32[64,16,1024]{2,0,1:T(8,128)S(1)} copy(f32[64,16,1024]{2,1,0:T(8,128)} %param.4) | data formatting | bytes 8388608 | tf_op args[0]
  12.1 4.0 %collective-permute-start.1 = (f32[64,1,1024]{2,0,1:T(8,128)S(1)}, f32[64,1,1024]{2,0,1:T(8,128)S(1)}, u32[]{:S(2)}, u32[]{:S(2)}) collective-permute-start(f32[64,1,1024]{2,0,1:T(8,128)S(1)} %get-tuple-element.15), channel_id=1, source_target_pairs={{0,8},{8,16},{16,24},{24,32},{32,40},{40,48},{48,56},{56,64},{64,7... | collective-permute-start | bytes 786440 | tf_op jit(solution)/shard_map/ppermute | solution.py:16
  16.0 1.3 collective-permute-start
  17.3 3.6 collective-permute-done.1
  21.0 2.4 constant_dynamic-update-slice_fusion.1
  23.5 0.0 copy-start.9
  23.5 1.3 collective-permute-done
  24.8 0.0 copy-start.7
  24.8 2.2 copy-done.7
  27.0 0.2 fusion.21
  27.2 0.2 copy.37
  27.5 3.8 collective-permute-start.2
  31.2 0.2 copy.39
  31.5 3.1 collective-permute-start.3
  34.6 0.3 copy.38
  34.9 0.5 collective-permute-done.3
  35.4 0.3 copy.40
  35.6 14.0 %fusion.11 = (f32[64,16,1024]{2,0,1:T(8,128)S(1)}, f32[64,16,1024]{2,0,1:T(8,128)}) fusion(f32[64,16,1024]{2,0,1:T(8,128)} %copy-done.6, f32[64,18,1024]{2,0,1:T(8,128)} %copy-done.7, f32[64,18,1]{2,0,1:T(8,128)S(1)} %copy.40, f32[64,18,1]{2,0,1:T(8,128)S(1)} %copy.38, f32[64,1,1024]{2,0,1:T(8,128)S(1)} %collective-permute-done.1, ...), kind=kOutput, calls=%fused_computation.22 | convolution fusion | flops 65011968 | bytes 18162944 | tf_op jit(solution)/shard_map/sc,cxy->sxy/dot_general | solution.py:30
  49.7 3.1 collective-permute-start.5
  52.8 1.3 collective-permute-start.4
  54.1 4.6 %collective-permute-done.5 = f32[64,1,1024]{2,0,1:T(8,128)S(1)} collective-permute-done((f32[64,1,1024]{2,0,1:T(8,128)S(1)}, f32[64,1,1024]{2,0,1:T(8,128)S(1)}, u32[]{:S(2)}, u32[]{:S(2)}) %collective-permute-start.5) | collective-permute-done | bytes 262176 | tf_op jit(solution)/shard_map/ppermute | solution.py:16
  58.7 4.2 %collective-permute-done.4 = f32[64,1,1024]{2,0,1:T(8,128)S(1)} collective-permute-done((f32[64,1,1024]{2,0,1:T(8,128)S(1)}, f32[64,1,1024]{2,0,1:T(8,128)S(1)}, u32[]{:S(2)}, u32[]{:S(2)}) %collective-permute-start.4) | collective-permute-done | bytes 262176 | tf_op jit(solution)/shard_map/ppermute | solution.py:17
  62.9 0.2 pad_maximum_fusion.15
  63.2 0.2 copy.44
  63.4 2.4 collective-permute-start.6
  65.8 0.2 copy.46
  66.0 3.6 collective-permute-start.7
  69.7 0.3 copy.45
  70.0 0.0 collective-permute-done.7
  70.0 0.3 copy.47
  70.3 10.7 %fusion.4 = f32[64,16,1024]{2,0,1:T(8,128)S(1)} fusion(f32[64,16,1024]{2,0,1:T(8,128)} %copy-done.2, f32[64,18,1]{2,0,1:T(8,128)S(1)} %copy.47, f32[64,1,1024]{2,0,1:T(8,128)S(1)} %collective-permute-done.4, f32[64,1,1024]{2,0,1:T(8,128)S(1)} %collective-permute-done.5, f32[64,18,1]{2,0,1:T(8,128)S(1)} %copy.45, f32[64,16,1024]{2,0,1:T(8,128)} %get-tuple-element.19, ...), kind=kLoop, calls=%fused_computation.7 | loop fusion | flops 18874368 | bytes 13181952 | tf_op jit(solution)/shard_map/sub | solution.py:26
  81.0 2.0 copy-done.4
  83.0 7.3 %convolution_bitcast_fusion = f32[128,128]{0,1:T(8,128)} fusion(f32[64,16,1024]{2,0,1:T(8,128)S(1)} %fusion.4, f32[64,16,1024]{2,0,1:T(8,128)S(1)} %copy-done.3), kind=kOutput, calls=%fused_computation.28 | convolution fusion | flops 3223322624 | bytes 8454144 | tf_op jit(solution)/shard_map/dot_general | solution.py:34
  90.2 0.0 all-reduce.2.cloned.1.call-update
  90.3 8.5 %pad_maximum_fusion = f32[128,16,1024]{2,0,1:T(8,128)} fusion(f32[64,16,1024]{2,0,1:T(8,128)} %copy-done.4, f32[64,16,1024]{2,0,1:T(8,128)} %copy-done.2), kind=kLoop, calls=%fused_computation.1 | loop fusion | flops 2097152 | bytes 16777216 | tf_op jit(solution)/shard_map/concatenate | solution.py:54
  98.8 9.4 %copy.50 = f32[128,16,1024]{0,2,1:T(8,128)} copy(f32[128,16,1024]{2,0,1:T(8,128)} %pad_maximum_fusion) | data formatting | bytes 16777216 | tf_op jit(solution)/shard_map/concatenate | solution.py:54
  108.2 228.0 %all-reduce.2.cloned.1.call-done = f32[128,128]{0,1:T(8,128)} async-done(((f32[128,128]{0,1:T(8,128)}), f32[128,128]{0,1:T(8,128)}) %all-reduce.2.cloned.1.call-update) | async-done | bytes 65552 | tf_op jit(solution)/shard_map/psum | solution.py:55
  336.3 0.9 copy.49
  337.2 0.9 fusion.17
  338.1 11.7 %cholesky.16 = f32[128,128]{1,0:T(8,128)S(1)} custom-call(f32[128,128]{1,0:T(8,128)S(1)} %fusion.17), custom_call_target="Cholesky" | custom-call | tf_op jit(solution)/shard_map/jit(cholesky)/cholesky | solution.py:56
  349.8 0.6 compare_reduce_fusion
  350.5 0.7 multiply_bitcast_fusion
  351.1 0.7 copy.51
  351.8 9.8 %custom-call.7 = f32[1,128,128]{1,2,0:T(8,128)S(1)} custom-call(f32[1,128,128]{2,1,0:T(8,128)S(1)} %get-tuple-element.17), custom_call_target="InvertDiagBlocksLowerTriangular" | custom-call | tf_op jit(solution)/shard_map/jit(_solve_triangular)/triangular_solve | solution.py:57
  361.7 10.8 %convolution_multiply_fusion = f32[128,16384]{1,0:T(8,128)S(1)} fusion(f32[128,16384]{0,1:T(8,128)} %bitcast.22, f32[1,128,128]{1,2,0:T(8,128)S(1)} %custom-call.7), kind=kOutput, calls=%fused_computation | convolution fusion | flops 3223322624 | bytes 16842752 | tf_op jit(solution)/shard_map/jit(_solve_triangular)/triangular_solve | solution.py:57
  372.5 9.9 %copy.54 = f32[16,8,16,1024]{3,2,1,0:T(8,128)} copy(f32[16,8,16,1024]{3,1,2,0:T(8,128)S(1)} %bitcast.23) | data formatting | bytes 16777216
  (22 shorter events, 0.2 us)
Async XLA Ops:
  7.2 28.5 %copy-start = (f32[4,16,1024]{2,1,0:T(8,128)S(1)}, f32[4,16,1024]{2,1,0:T(8,128)}, u32[]{:S(2)}) copy-start(f32[4,16,1024]{2,1,0:T(8,128)} %param.5) | copy-start | bytes 786436
  7.2 329.1 %all-reduce.2.cloned.1.call-start = ((), (), s32[]{:S(2)}) async-start(), calls=%async_computation | async-start | bytes 131072 | tf_op jit(solution)/shard_map/psum | solution.py:55
  7.2 13.8 %copy-start.5 = (f32[64,16,1024]{2,1,0:T(8,128)S(1)}, f32[64,16,1024]{2,1,0:T(8,128)}, u32[]{:S(2)}) copy-start(f32[64,16,1024]{2,1,0:T(8,128)} %param.4) | copy-start | bytes 12582916
  12.0 11.4 %copy-start.6 = (f32[64,16,1024]{2,0,1:T(8,128)}, f32[64,16,1024]{2,0,1:T(8,128)S(1)}, u32[]{:S(2)}) copy-start(f32[64,16,1024]{2,0,1:T(8,128)S(1)} %copy.42) | copy-start | bytes 12582916
  12.1 8.9 %collective-permute-start.1 = (f32[64,1,1024]{2,0,1:T(8,128)S(1)}, f32[64,1,1024]{2,0,1:T(8,128)S(1)}, u32[]{:S(2)}, u32[]{:S(2)}) collective-permute-start(f32[64,1,1024]{2,0,1:T(8,128)S(1)} %get-tuple-element.15), channel_id=1, source_target_pairs={{0,8},{8,16},{16,24},{24,32},{32,40},{40,48},{48,56},{56,64},{64,7... | collective-permute-start | bytes 786440 | tf_op jit(solution)/shard_map/ppermute | solution.py:16
  16.0 8.8 %collective-permute-start = (f32[64,1,1024]{2,0,1:T(8,128)S(1)}, f32[64,1,1024]{2,0,1:T(8,128)S(1)}, u32[]{:S(2)}, u32[]{:S(2)}) collective-permute-start(f32[64,1,1024]{2,0,1:T(8,128)S(1)} %get-tuple-element.14), channel_id=1, source_target_pairs={{8,0},{16,8},{24,16},{32,24},{40,32},{48,40},{56,48},{64,56},{72,6... | collective-permute-start | bytes 786440 | tf_op jit(solution)/shard_map/ppermute | solution.py:17
  23.5 12.2 %copy-start.8 = (f32[16,1024]{1,0:T(8,128)S(1)}, f32[16,1024]{1,0:T(8,128)}, u32[]{:S(2)}) copy-start(f32[16,1024]{1,0:T(8,128)} %param.6) | copy-start | bytes 196612
  23.5 12.2 %copy-start.9 = (s32[64]{0:T(128)S(1)}, s32[64]{0:T(128)}, u32[]{:S(2)}) copy-start(s32[64]{0:T(128)} %param.7) | copy-start | bytes 772
  24.8 2.2 copy-start.7
  27.5 7.1 %collective-permute-start.2 = (f32[64,18,1]{0,2,1:T(1,128)S(1)}, f32[64,18,1]{0,2,1:T(1,128)S(1)}, u32[]{:S(2)}, u32[]{:S(2)}) collective-permute-start(f32[64,18,1]{0,2,1:T(1,128)S(1)} %copy.37), channel_id=1, source_target_pairs={{1,0},{2,1},{3,2},{4,3},{5,4},{6,5},{7,6},{9,8},{10,9},{11,10},{12... | collective-permute-start | bytes 13832 | tf_op jit(solution)/shard_map/ppermute | solution.py:17
  31.5 3.9 %collective-permute-start.3 = (f32[64,18,1]{0,2,1:T(1,128)S(1)}, f32[64,18,1]{0,2,1:T(1,128)S(1)}, u32[]{:S(2)}, u32[]{:S(2)}) collective-permute-start(f32[64,18,1]{0,2,1:T(1,128)S(1)} %copy.39), channel_id=1, source_target_pairs={{0,1},{1,2},{2,3},{3,4},{4,5},{5,6},{6,7},{8,9},{9,10},{10,11},{11... | collective-permute-start | bytes 13832 | tf_op jit(solution)/shard_map/ppermute | solution.py:16
  49.6 13.3 %copy-start.2 = (f32[64,16,1024]{2,0,1:T(8,128)}, f32[64,16,1024]{2,0,1:T(8,128)S(1)}, u32[]{:S(2)}) copy-start(f32[64,16,1024]{2,0,1:T(8,128)S(1)} %get-tuple-element.18) | copy-start | bytes 12582916
  49.7 9.0 %collective-permute-start.5 = (f32[64,1,1024]{2,0,1:T(8,128)S(1)}, f32[64,1,1024]{2,0,1:T(8,128)S(1)}, u32[]{:S(2)}, u32[]{:S(2)}) collective-permute-start(f32[64,1,1024]{2,0,1:T(8,128)S(1)} %get-tuple-element.12), channel_id=1, source_target_pairs={{0,8},{8,16},{16,24},{24,32},{32,40},{40,48},{48,56},{56,64},{64,7... | collective-permute-start | bytes 786440 | tf_op jit(solution)/shard_map/ppermute | solution.py:16
  52.8 10.1 %collective-permute-start.4 = (f32[64,1,1024]{2,0,1:T(8,128)S(1)}, f32[64,1,1024]{2,0,1:T(8,128)S(1)}, u32[]{:S(2)}, u32[]{:S(2)}) collective-permute-start(f32[64,1,1024]{2,0,1:T(8,128)S(1)} %get-tuple-element.13), channel_id=1, source_target_pairs={{8,0},{16,8},{24,16},{32,24},{40,32},{48,40},{56,48},{64,56},{72,6... | collective-permute-start | bytes 786440 | tf_op jit(solution)/shard_map/ppermute | solution.py:17
  63.4 6.3 %collective-permute-start.6 = (f32[64,18,1]{0,2,1:T(1,128)S(1)}, f32[64,18,1]{0,2,1:T(1,128)S(1)}, u32[]{:S(2)}, u32[]{:S(2)}) collective-permute-start(f32[64,18,1]{0,2,1:T(1,128)S(1)} %copy.44), channel_id=1, source_target_pairs={{1,0},{2,1},{3,2},{4,3},{5,4},{6,5},{7,6},{9,8},{10,9},{11,10},{12... | collective-permute-start | bytes 13832 | tf_op jit(solution)/shard_map/ppermute | solution.py:17
  66.0 4.0 %collective-permute-start.7 = (f32[64,18,1]{0,2,1:T(1,128)S(1)}, f32[64,18,1]{0,2,1:T(1,128)S(1)}, u32[]{:S(2)}, u32[]{:S(2)}) collective-permute-start(f32[64,18,1]{0,2,1:T(1,128)S(1)} %copy.46), channel_id=1, source_target_pairs={{0,1},{1,2},{2,3},{3,4},{4,5},{5,6},{6,7},{8,9},{9,10},{10,11},{11... | collective-permute-start | bytes 13832 | tf_op jit(solution)/shard_map/ppermute | solution.py:16
  70.3 12.7 %copy-start.3 = (f32[64,16,1024]{2,0,1:T(8,128)S(1)}, f32[64,16,1024]{2,0,1:T(8,128)}, u32[]{:S(2)}) copy-start(f32[64,16,1024]{2,0,1:T(8,128)} %copy-done.2) | copy-start | bytes 12582916
  81.0 2.0 copy-start.4
  372.5 9.9 %copy-start.1 = (f32[4,16,1024]{2,1,0:T(8,128)S(1)}, f32[4,16,1024]{2,1,0:T(8,128)}, u32[]{:S(2)}) copy-start(f32[4,16,1024]{2,1,0:T(8,128)} %param.5) | copy-start | bytes 786436
Sparse Core Ops, SparseCore 0:
  90.4 245.8 all-reduce.1
where the time goes:
time: 397 us; the launch traced here: 389 us
  waiting for transfers between devices  242 us (61%)
  other arithmetic  43.2 us (11%)
  local copies, waits for them, and re-layouts  34.7 us (9%)
  matrix products  32.1 us (8%)
  starting transfers between devices  22.6 us (6%)
  between operations  14.6 us (4%)
    psum x1, waiting for transfers between devices, shards(): total = lax.psum(gram_matrix(snapshots), ('wide', 'narrow'))  228 us
    unnamed x25, local copies, waits for them, and re-layouts  22 us
    dot_general x1, matrix products, select_fields(): jnp.einsum('sc,cxy->sxy', onehot, table, precision=lax.Precision.HIGHEST)  14 us
    ppermute x4, starting transfers between devices, with_halo(): before = lax.ppermute(last, axis, up)  13.8 us
    another operation x3, other arithmetic, shards(): lower_chol = jnp.linalg.cholesky(total)  12.4 us
    another operation x1, matrix products, shards(): jax.scipy.linalg.solve_triangular(lower_chol, snapshots, lower=True)  10.8 us
    sub x1, other arithmetic, advance(): state + 0.2 * coefficient * (neighbours - 4.0 * state) - decay * state  10.7 us
    another operation x1, other arithmetic, shards(): jax.scipy.linalg.solve_triangular(lower_chol, snapshots, lower=True)  9.81 us
  transfers between devices with their start and end apart: 9, of which 6 were waited for; matrix products, arithmetic and copies ran while one was open for 5% of the time, Pallas kernels for 0%

commit v1 on v0

v1 whole, which is shorter than its diff:
```python
import math

import jax
import jax.numpy as jnp
from jax import lax
from jax.experimental import pallas as pl
from jax.experimental.pallas import tpu as pltpu
from jax.sharding import Mesh, PartitionSpec as P

F32, BF16 = jnp.float32, jnp.bfloat16
S, ROWS, COLS, FIELDS = 64, 16, 1024, 4
SNAP = 2 * S
TILES, GROUPS = COLS // 128, S // 8
EXT = S + 8
KAP, DEC = S, S + FIELDS
BLOCK = 16
ROWAXIS, COLAXIS = ("z", "x"), ("y", "core")
ANY = pl.BlockSpec(memory_space=pl.ANY)
VM = pl.BlockSpec(memory_space=pltpu.VMEM)
VMEM_LIMIT = 24 * 2**20


def params():
    return pltpu.CompilerParams(vmem_limit_bytes=VMEM_LIMIT)


def lanes():
    return lax.broadcasted_iota(jnp.int32, (8, 128), 1)


def tile(t):
    return slice(128 * t, 128 * t + 128)


def group(g):
    return slice(8 * g, 8 * g + 8)


def pack_kernel(u, kap, dec, uall, north, south, west, east, sems):
    for x in range(ROWS):
        uall[x, S:EXT, :] = jnp.zeros((8, COLS), F32)
    order = [0, ROWS - 1] + list(range(1, ROWS - 1))
    copies = {}
    for x in order:
        copies[x] = (
            pltpu.make_async_copy(u.at[:, x, :], uall.at[x, 0:S, :], sems.at[0, x]),
            pltpu.make_async_copy(kap.at[:, x, :], uall.at[x, KAP : KAP + FIELDS, :], sems.at[1, x]),
            pltpu.make_async_copy(dec.at[x : x + 1, :], uall.at[x, DEC : DEC + 1, :], sems.at[2, x]),
        )
        for copy in copies[x]:
            copy.start()
    lane = lanes()
    w = [jnp.zeros((8, 128), F32) for _ in range(GROUPS + 1)]
    e = [jnp.zeros((8, 128), F32) for _ in range(GROUPS + 1)]
    for x in order:
        for copy in copies[x]:
            copy.wait()
        if x == 0:
            north[...] = uall[0]
        if x == ROWS - 1:
            south[...] = uall[ROWS - 1]
        for g in range(GROUPS + 1):
            first, last = uall[x, group(g), tile(0)], uall[x, group(g), tile(TILES - 1)]
            w[g] = jnp.where(lane == x, pltpu.roll(first, x, 1), w[g])
            w[g] = jnp.where(lane == ROWS + x, pltpu.roll(first, ROWS + x - 1, 1), w[g])
            e[g] = jnp.where(lane == x, pltpu.roll(last, x + 1, 1), e[g])
            e[g] = jnp.where(lane == ROWS + x, pltpu.roll(last, ROWS + x + 2, 1), e[g])
    for g in range(GROUPS + 1):
        west[group(g), :] = w[g]
        east[group(g), :] = e[g]


def pack(initial, kappa, decay):
    row, col = pltpu.VMEM((EXT, COLS), F32), pltpu.VMEM((EXT, 128), F32)
    return pl.pallas_call(
        pack_kernel,
        name="pack",
        in_specs=[ANY] * 3,
        out_specs=[VM] * 5,
        out_shape=[pltpu.VMEM((ROWS, EXT, COLS), F32), row, row, col, col],
        scratch_shapes=[pltpu.SemaphoreType.DMA((3, ROWS))],
        compiler_params=params(),
    )(initial, kappa, decay)


def field_rows(load, t):
    k = [jnp.broadcast_to(load(KAP + c, t), (8, 128)) * 0.2 for c in range(FIELDS)]
    return k, 1.0 - jnp.broadcast_to(load(DEC, t), (8, 128))


def choose(k, f):
    odd = (f & 1) == 1
    return jnp.where((f & 2) == 2, jnp.where(odd, k[3], k[2]), jnp.where(odd, k[1], k[0]))


def step_row(fi, load_field, center, above, below, edge_w, edge_e, emit):
    lane = lanes()
    low, high = lane == 0, lane == 127
    from_w = [edge_w(g) for g in range(GROUPS)]
    from_e = [pltpu.roll(center(g, 0), 127, 1) for g in range(GROUPS)]
    for t in range(TILES):
        k, keep = field_rows(load_field, t)
        held = None
        for g in range(GROUPS):
            here = center(g, t)
            right = pltpu.roll(here, 1, 1)
            west = jnp.where(low, from_w[g], right)
            from_w[g] = right
            nxt = pltpu.roll(center(g, t + 1), 127, 1) if t + 1 < TILES else edge_e(g)
            east = jnp.where(high, nxt, from_e[g])
            from_e[g] = nxt
            b = choose(k, fi[group(g), :])
            a = keep - 4.0 * b
            new = a * here + b * ((above(g, t) + below(g, t)) + (west + east))
            if g % 2 == 0:
                held = new
            else:
                emit(g - 1, t, held, new)


def split_store(hi, lo, index, base, g, t, first, second):
    both = jnp.concatenate([first, second], 0)
    top = both.astype(BF16)
    rest = (both - top.astype(F32)).astype(BF16)
    where = slice(base + 8 * g, base + 8 * g + 16)
    hi[index, where, tile(t)] = top
    lo[index, where, tile(t)] = rest


def gram(acc, hi, lo):
    rhs = jnp.concatenate([hi, lo], 0)
    acc[...] += lax.dot_general(hi, rhs, (((1,), (1,)), ((), ())), preferred_element_type=F32)


def column_step(fi, halo, own, g, up=None, down=None):
    lane = lanes()
    one = halo[group(g), :]
    two = pltpu.roll(one, 128 - ROWS, 1)
    k = [jnp.broadcast_to(halo[KAP + c : KAP + c + 1, :], (8, 128)) * 0.2 for c in range(FIELDS)]
    keep = 1.0 - jnp.broadcast_to(halo[DEC : DEC + 1, :], (8, 128))
    b = choose(k, fi[group(g), :])
    above, below = pltpu.roll(one, 1, 1), pltpu.roll(one, 127, 1)
    if up is not None:
        above = jnp.where(lane == 0, up, above)
        below = jnp.where(lane == ROWS - 1, down, below)
    return (keep - 4.0 * b) * one + b * ((above + below) + (two + own[group(g), :]))


def interior_kernel(fi, uall, own_w, own_e, halo_w, halo_e, first, hi, lo, acc, col_w, col_e):
    acc[...] = jnp.zeros_like(acc)
    for g in range(GROUPS):
        col_w[group(g), :] = column_step(fi, halo_w, own_w, g)
        col_e[group(g), :] = column_step(fi, halo_e, own_e, g)

    def field(x):
        return lambda r, t: uall[x, r : r + 1, tile(t)]

    def one(x, keep):
        def emit(g, t, p, q):
            first[x, group(g), tile(t)] = p
            first[x, group(g + 1), tile(t)] = q
            if keep:
                split_store(hi, lo, x - 2, 0, g, t, p, q)

        step_row(
            fi,
            field(x),
            lambda g, t: uall[x, group(g), tile(t)],
            lambda g, t: uall[x - 1, group(g), tile(t)],
            lambda g, t: uall[x + 1, group(g), tile(t)],
            lambda g: pltpu.roll(halo_w[group(g), :], (128 - x) % 128, 1),
            lambda g: pltpu.roll(halo_e[group(g), :], 127 - x, 1),
            emit,
        )

    def two(x):
        step_row(
            fi,
            field(x),
            lambda g, t: first[x, group(g), tile(t)],
            lambda g, t: first[x - 1, group(g), tile(t)],
            lambda g, t: first[x + 1, group(g), tile(t)],
            lambda g: pltpu.roll(col_w[group(g), :], (128 - x) % 128, 1),
            lambda g: pltpu.roll(col_e[group(g), :], 127 - x, 1),
            lambda g, t, p, q: split_store(hi, lo, x - 2, S, g, t, p, q),
        )

    one(1, False)
    one(2, True)

    def body(x, carry):
        one(x, True)
        two(x - 1)
        gram(acc, hi[x - 3], lo[x - 3])
        return carry

    lax.fori_loop(3, ROWS - 2, body, 0)
    one(ROWS - 2, False)
    two(ROWS - 3)
    gram(acc, hi[ROWS - 5], lo[ROWS - 5])


def interior(fi, uall, own_w, own_e, halo_w, halo_e):
    snap = pltpu.VMEM((ROWS - 4, SNAP, COLS), BF16)
    return pl.pallas_call(
        interior_kernel,
        name="interior",
        in_specs=[VM] * 6,
        out_specs=[VM] * 4,
        out_shape=[pltpu.VMEM((ROWS, S, COLS), F32), snap, snap, pltpu.VMEM((SNAP, 2 * SNAP), F32)],
        scratch_shapes=[pltpu.VMEM((S, 128), F32)] * 2,
        cost_estimate=pl.CostEstimate(flops=2 * 12 * SNAP * 2 * SNAP * COLS, bytes_accessed=2**25, transcendentals=0),
        compiler_params=params(),
    )(fi, uall, own_w, own_e, halo_w, halo_e)


def edge_kernel(
    fi, uall, own_w, own_e, halo_w, halo_e, first, inner, n1, s1, n2, s2, hi, lo, packed, col_w, col_e, edge, acc
):
    acc[...] = inner[...]
    lane = lanes()
    corner = slice(COLS, COLS + 128)
    for g in range(GROUPS):
        up, down = n2[group(g), corner], s2[group(g), corner]
        col_w[group(g), :] = column_step(fi, halo_w, own_w, g, up, pltpu.roll(down, ROWS - 1, 1))
        col_e[group(g), :] = column_step(fi, halo_e, own_e, g, pltpu.roll(up, 127, 1), pltpu.roll(down, ROWS - 2, 1))

    def rows(ref):
        return lambda g, t: ref[group(g), tile(t)]

    def at(ref, x):
        return lambda g, t: ref[x, group(g), tile(t)]

    def field(x):
        return lambda r, t: uall[x, r : r + 1, tile(t)]

    def pick(ref, x, to):
        return lambda g: pltpu.roll(ref[group(g), :], (to - x) % 128, 1)

    last = ROWS - 1
    for near, far, row, inside, slot, beyond in ((n1, n2, 0, 1, 0, 2), (s1, s2, last, last - 1, 2, 3)):

        def put(index):
            def emit(g, t, p, q):
                edge[index, group(g), tile(t)] = p
                edge[index, group(g + 1), tile(t)] = q

            return emit

        def put_both(index, target):
            def emit(g, t, p, q):
                put(index)(g, t, p, q)
                split_store(hi, lo, target, 0, g, t, p, q)

            return emit

        def put_second(target):
            return lambda g, t, p, q: split_store(hi, lo, target, S, g, t, p, q)

        outer = 0 if row == 0 else 3
        inner_slot = 1 if row == 0 else 2
        step_row(
            fi,
            lambda r, t, near=near: near[r : r + 1, tile(t)],
            rows(near),
            rows(far),
            at(uall, row),
            pick(far_corner(far), 0, 0),
            pick(far_corner(far), 1, 127),
            put(0),
        )
        step_row(
            fi, field(row), at(uall, row), rows(near), at(uall, inside),
            pick(halo_w, row, 0), pick(halo_e, row, 127), put_both(1, outer),
        )
        step_row(
            fi, field(row), at(edge, 1), at(edge, 0), at(first, inside),
            pick(col_w, row, 0), pick(col_e, row, 127), put_second(outer),
        )
        deeper = inside + (inside - row)
        step_row(
            fi, field(inside), at(first, inside), at(edge, 1), at(first, deeper),
            pick(col_w, inside, 0), pick(col_e, inside, 127), put_second(inner_slot),
        )
        for t in range(TILES):
            for g in range(0, GROUPS, 2):
                split_store(
                    hi, lo, inner_slot, 0, g, t,
                    first[inside, group(g), tile(t)], first[inside, group(g + 1), tile(t)],
                )
        gram(acc, hi[outer], lo[outer])
        gram(acc, hi[inner_slot], lo[inner_slot])
    cross = acc[:, SNAP:]
    full = acc[:, :SNAP] + (cross + cross.T)
    top, bottom = full[:S, :], pltpu.roll(full[S:, :], S, 1)
    r = lax.broadcasted_iota(jnp.int32, (S, SNAP), 0)
    c = lax.broadcasted_iota(jnp.int32, (S, SNAP), 1)
    packed[0:S, :] = jnp.where((c < S) & (r > c), bottom, top)
    diag = jnp.sum(jnp.where(r == c, bottom, 0.0), axis=0, keepdims=True)
    packed[S : S + 8, :] = jnp.where(lax.broadcasted_iota(jnp.int32, (8, SNAP), 0) == 0, diag, 0.0)
    packed[S + 8 :, :] = jnp.zeros((8, SNAP), F32)


def far_corner(ref):
    return ref.at[:, COLS : COLS + 128]


def edges(fi, uall, own_w, own_e, halo_w, halo_e, first, inner, n1, s1, n2, s2):
    snap = pltpu.VMEM((4, SNAP, COLS), BF16)
    return pl.pallas_call(
        edge_kernel,
        name="edges",
        in_specs=[VM] * 12,
        out_specs=[VM] * 3,
        out_shape=[snap, snap, pltpu.VMEM((S + 16, SNAP), F32)],
        scratch_shapes=[
            pltpu.VMEM((S, 128), F32),
            pltpu.VMEM((S, 128), F32),
            pltpu.VMEM((2, S, COLS), F32),
            pltpu.VMEM((SNAP, 2 * SNAP), F32),
        ],
        compiler_params=params(),
    )(fi, uall, own_w, own_e, halo_w, halo_e, first, inner, n1, s1, n2, s2)


def unpack(packed):
    top, diag = packed[0:S, :], packed[S : S + 1, :]
    r = lax.broadcasted_iota(jnp.int32, (S, SNAP), 0)
    c = lax.broadcasted_iota(jnp.int32, (S, SNAP), 1)
    upper = jnp.where(r <= c, top, 0.0)
    lower = pltpu.roll(jnp.where((r > c) & (c < S), top, 0.0), S, 1)
    on_diag = jnp.where(r == c - S, pltpu.roll(jnp.broadcast_to(diag, (8, SNAP)), S, 1)[0:1, :], 0.0)
    zero = jnp.zeros_like(lower)
    return jnp.concatenate([upper, on_diag], 0) + jnp.concatenate([zero, lower], 0).T


def factor(m, z):
    sub = lax.broadcasted_iota(jnp.int32, (8, 128), 0)
    for k in range(SNAP // BLOCK):
        lo = k * BLOCK
        panel = m[lo : lo + BLOCK, :]
        p = {}
        for i in range(BLOCK):
            for j in range(i, BLOCK):
                p[i, j] = jnp.broadcast_to(panel[i : i + 1, lo + j : lo + j + 1], (8, 128))
        rows = [[jnp.broadcast_to(panel[i : i + 1, tile(h)], (8, 128)) for h in range(2)] for i in range(BLOCK)]
        for j in range(BLOCK):
            r = lax.rsqrt(p[j, j])
            u = {i: p[j, i] * r for i in range(j + 1, BLOCK)}
            for i in range(j + 1, BLOCK):
                for l in range(i, BLOCK):
                    p[i, l] = p[i, l] - u[i] * u[l]
            rows[j] = [v * r for v in rows[j]]
            for i in range(j + 1, BLOCK):
                rows[i] = [v - u[i] * w for v, w in zip(rows[i], rows[j])]
        for part in range(BLOCK // 8):
            for h in range(2):
                v = rows[8 * part][h]
                for i in range(1, 8):
                    v = jnp.where(sub == i, rows[8 * part + i][h], v)
                z[lo + 8 * part : lo + 8 * part + 8, tile(h)] = v
        if lo + BLOCK < SNAP:
            done = z[lo : lo + BLOCK, :]
            update = lax.dot_general(
                done[:, :SNAP], done, (((0,), (0,)), ((), ())),
                precision=lax.Precision.HIGHEST, preferred_element_type=F32,
            )
            m[lo + BLOCK :, :] = m[lo + BLOCK :, :] - update[lo + BLOCK :, :]


def basis_kernel(scale, packed, hi, lo, ehi, elo, out, tri, m, z, buf, sems):
    r = lax.broadcasted_iota(jnp.int32, (SNAP, SNAP), 0)
    c = lax.broadcasted_iota(jnp.int32, (SNAP, SNAP), 1)
    m[:, :SNAP] = unpack(packed)
    m[:, SNAP:] = jnp.where(r == c, 1.0, 0.0)
    factor(m, z)
    tri[...] = jnp.where(r <= c, z[:, :SNAP], 0.0) * (1.0 / scale)
    w = jnp.where(r >= c, z[:, SNAP:], 0.0) * scale
    top = w.astype(BF16)
    rest = (w - top.astype(F32)).astype(BF16)
    lhs = jnp.concatenate([jnp.concatenate([top, top], 1), jnp.concatenate([rest, rest], 1)], 0)

    def copy(x):
        return pltpu.make_async_copy(buf.at[x], out.at[:, x, :], sems.at[x])

    def row(x, h, l):
        both = jnp.dot(lhs, jnp.concatenate([h, l], 0), preferred_element_type=F32)
        buf[x] = both[:SNAP] + both[SNAP:]
        copy(x).start()

    def body(i, carry):
        row(i + 2, hi[i], lo[i])
        return carry

    lax.fori_loop(0, ROWS - 4, body, 0)
    for i, x in enumerate((0, 1, ROWS - 2, ROWS - 1)):
        row(x, ehi[i], elo[i])
    for x in range(ROWS):
        copy(x).wait()


def make_basis(scale, packed, hi, lo, ehi, elo):
    def kernel(*refs):
        basis_kernel(scale, *refs)

    return pl.pallas_call(
        kernel,
        name="basis",
        in_specs=[VM] * 5,
        out_specs=[ANY, VM],
        out_shape=[
            jax.ShapeDtypeStruct((SNAP, ROWS, COLS), F32),
            jax.ShapeDtypeStruct((SNAP, SNAP), F32),
        ],
        scratch_shapes=[
            pltpu.VMEM((SNAP, 2 * SNAP), F32),
            pltpu.VMEM((SNAP, 2 * SNAP), F32),
            pltpu.VMEM((ROWS, SNAP, COLS), F32),
            pltpu.SemaphoreType.DMA((ROWS,)),
        ],
        compiler_params=params(),
    )(packed, hi, lo, ehi, elo)


def spread_sum(value, axis):
    count = lax.axis_size(axis)
    return lax.all_to_all(jnp.broadcast_to(value[None], (count, *value.shape)), axis, 0, 0).sum(0)


def sum_over_devices(packed):
    swap = [(0, 1), (1, 0)]
    second = lax.axis_index("core") == 1
    half = packed.shape[0] // 2
    a, b = packed[:half], packed[half:]
    mine = jnp.where(second, b, a) + lax.ppermute(jnp.where(second, a, b), "core", swap)
    mine = spread_sum(mine, ("x", "y"))
    mine = spread_sum(mine, "z")
    other = lax.ppermute(mine, "core", swap)
    return jnp.concatenate([jnp.where(second, other, mine), jnp.where(second, mine, other)], 0)


def along(axis):
    count = lax.axis_size(axis)
    return [(i, i + 1) for i in range(count - 1)], [(i + 1, i) for i in range(count - 1)]


def shards(initial, kappa, decay, field_index):
    fi = jnp.broadcast_to(field_index[:, None], (S, 128))
    uall, north, south, own_w, own_e = pack(initial, kappa, decay)
    up, down = along(ROWAXIS), along(COLAXIS)
    halo_w = lax.ppermute(own_e, COLAXIS, down[0])
    halo_e = lax.ppermute(own_w, COLAXIS, down[1])
    n1 = lax.ppermute(south, ROWAXIS, up[0])
    s1 = lax.ppermute(north, ROWAXIS, up[1])

    def far(row, edge_row):
        pad = jnp.zeros((S, 126), F32)
        ends = [h[:S, edge_row : edge_row + 1] for h in (halo_w, halo_e)]
        return jnp.concatenate([uall[row, :S, :], *ends, pad], 1)

    n2 = lax.ppermute(far(ROWS - 2, ROWS - 1), ROWAXIS, up[0])
    s2 = lax.ppermute(far(1, 0), ROWAXIS, up[1])
    first, hi, lo, inner = interior(fi, uall, own_w, own_e, halo_w, halo_e)
    ehi, elo, packed = edges(fi, uall, own_w, own_e, halo_w, halo_e, first, inner, n1, s1, n2, s2)
    total = sum_over_devices(packed)
    cells = lax.axis_size(ROWAXIS) * lax.axis_size(COLAXIS) * ROWS * COLS
    return make_basis(math.sqrt(cells), total, hi, lo, ehi, elo)


def solution(mesh):
    wide, narrow = mesh.devices.shape
    fine = Mesh(mesh.devices.reshape(wide // 4, 4, narrow // 2, 2), ("z", "x", "y", "core"))
    grid = P(None, ROWAXIS, COLAXIS)
    return jax.shard_map(
        shards,
        mesh=fine,
        in_specs=(grid, grid, P(ROWAXIS, COLAXIS), P()),
        out_specs=(grid, P()),
        check_vma=False,
    )
```

time: 397 us -> 112 us (0.28); the launches traced: 389 us -> 111 us
  waiting for transfers between devices: 242 us -> 2.04 us
  other arithmetic: 43.2 us -> 0.06 us
  blocking collectives: 0 us -> 36.6 us
  matrix products: 32.1 us -> 0 us
  Pallas kernels: 0 us -> 31.8 us
  local copies, waits for them, and re-layouts: 34.7 us -> 19.1 us
  between operations: 14.6 us -> 0.98 us
    psum x1 -> x0, waiting for transfers between devices: 228 us -> none  [shards(): total = lax.psum(gram_matrix(snapshots), ('wide', 'narrow'))]
    all_to_all x0 -> x2, blocking collectives: none -> 36.6 us  [spread_sum(): lax.all_to_all(jnp.broadcast_to(value[None], (count, *value.shape)), axis...]
    pallas_call x0 -> x4, Pallas kernels: none -> 31.8 us  [the longest x1 12.8 us: make_basis(): pl.pallas_call(kernel, name='basis', in_specs=[VM] * 5, out_specs=[ANY, V...]
    another operation x4 -> x0, other arithmetic: 22.2 us -> none  [the longest x3 12.4 us: shards(): lower_chol = jnp.linalg.cholesky(total)]
    dot_general x2 -> x0, matrix products: 21.3 us -> none  [the longest x1 14 us: select_fields(): jnp.einsum('sc,cxy->sxy', onehot, table, precision=lax.Precision.HIGHEST)]
    ppermute x8, waiting for transfers between devices: 14.3 us -> 2.04 us  [the longest x1 1.18 us: sum_over_devices(): lax.ppermute(jnp.where(second, a, b), 'core', swap)]
    another operation x1 -> x0, matrix products: 10.8 us -> none  [shards(): jax.scipy.linalg.solve_triangular(lower_chol, snapshots, lower=True)]
    sub x1 -> x0, other arithmetic: 10.7 us -> none  [advance(): state + 0.2 * coefficient * (neighbours - 4.0 * state) - decay * state]
  transfers between devices with their start and end apart: 9 -> 8, of which waited for: 6 -> 2; matrix products, arithmetic and copies ran while one was open for 5% -> 2% of each run, Pallas kernels for 0% -> 8%
where the time goes in v1:
time: 112 us; the launch traced here: 111 us
  blocking collectives  36.6 us (33%)
  Pallas kernels  31.8 us (28%)
  starting transfers between devices  20.7 us (18%)
  local copies, waits for them, and re-layouts  19.1 us (17%)
  waiting for transfers between devices  2.04 us (2%)
    all_to_all x2, blocking collectives, spread_sum(): lax.all_to_all(jnp.broadcast_to(value[None], (count, *value.shape)), axis...  36.6 us
    unnamed x30, local copies, waits for them, and re-layouts  17.2 us
    pallas_call x1, Pallas kernels, make_basis(): pl.pallas_call(kernel, name='basis', in_specs=[VM] * 5, out_specs=[ANY, V...  12.8 us
    pallas_call x1, Pallas kernels, interior(): pl.pallas_call(interior_kernel, name='interior', in_specs=[VM] * 6, out_s...  9.4 us
    pallas_call x1, Pallas kernels, pack(): pl.pallas_call(pack_kernel, name='pack', in_specs=[ANY] * 3, out_specs=[V...  6.07 us
    ppermute x1, starting transfers between devices, shards(): n2 = lax.ppermute(far(ROWS - 2, ROWS - 1), ROWAXIS, up[0])  4.69 us
    ppermute x1, starting transfers between devices, shards(): halo_w = lax.ppermute(own_e, COLAXIS, down[0])  4.59 us
    ppermute x1, starting transfers between devices, sum_over_devices(): other = lax.ppermute(mine, 'core', swap)  3.74 us
  transfers between devices with their start and end apart: 8, of which 2 were waited for; matrix products, arithmetic and copies ran while one was open for 2% of the time, Pallas kernels for 8%

profile of v1, /device:TPU:1, one launch (start us, length us, event | category | flops | bytes accessed | tf_op | source)
XLA Modules:
  0.0 111.2 jit_solution(2738797378299092214)
XLA Ops:
  0.6 0.0 copy-start.2
  0.6 2.2 %copy-done.2 = f32[64,16,1024]{2,1,0:T(8,128)S(1)} copy-done((f32[64,16,1024]{2,1,0:T(8,128)S(1)}, f32[64,16,1024]{2,1,0:T(8,128)}, u32[]{:S(2)}) %copy-start.2) | copy-done | bytes 4194328
  2.8 0.9 copy-done.9
  3.8 0.8 copy-done.13
  4.6 6.1 %pack.1 = (f32[16,72,1024]{2,1,0:T(8,128)S(1)}, f32[72,1024]{1,0:T(8,128)}, f32[72,1024]{1,0:T(8,128)}, f32[72,128]{1,0:T(8,128)S(1)}, f32[72,128]{1,0:T(8,128)S(1)}) custom-call(f32[64,16,1024]{2,1,0:T(8,128)S(1)} %copy-done.2, f32[4,16,1024]{2,1,0:T(8,128)S(1)} %copy-done.9, f32[16,1024]{1,0:T(8,128)S(1)} %copy-done.13), custom_call_target="tpu_custom_call" | custom-call | tf_op jit(solution)/shard_map/pack/pallas_call | solution.py:75
  10.7 0.0 copy-start.10
  10.7 4.6 %collective-permute-start = (f32[72,128]{1,0:T(8,128)S(1)}, f32[72,128]{1,0:T(8,128)S(1)}, u32[]{:S(2)}, u32[]{:S(2)}) collective-permute-start(f32[72,128]{1,0:T(8,128)S(1)} %get-tuple-element.16.own_e), channel_id=1, source_target_pairs={{0,1},{1,2},{2,3},{3,4},{4,5},{5,6},{6,7},{8,9},{9,10},{10,11},{11... | collective-permute-start | bytes 110600 | tf_op jit(solution)/shard_map/ppermute | solution.py:451
  15.3 1.9 %collective-permute-start.1 = (f32[72,128]{1,0:T(8,128)S(1)}, f32[72,128]{1,0:T(8,128)S(1)}, u32[]{:S(2)}, u32[]{:S(2)}) collective-permute-start(f32[72,128]{1,0:T(8,128)S(1)} %get-tuple-element.15.own_w), channel_id=1, source_target_pairs={{1,0},{2,1},{3,2},{4,3},{5,4},{6,5},{7,6},{9,8},{10,9},{11,10},{12... | collective-permute-start | bytes 110600 | tf_op jit(solution)/shard_map/ppermute | solution.py:452
  17.2 3.1 %collective-permute-start.2 = (f32[72,1024]{1,0:T(8,128)}, f32[72,1024]{1,0:T(8,128)S(1)}, u32[]{:S(2)}, u32[]{:S(2)}) collective-permute-start(f32[72,1024]{1,0:T(8,128)} %get-tuple-element.19), channel_id=1, source_target_pairs={{0,8},{8,16},{16,24},{24,32},{32,40},{40,48},{48,56},{56,64},{64,7... | collective-permute-start | bytes 884744 | tf_op jit(solution)/shard_map/ppermute | solution.py:453
  20.4 1.3 %collective-permute-start.3 = (f32[72,1024]{1,0:T(8,128)}, f32[72,1024]{1,0:T(8,128)}, u32[]{:S(2)}, u32[]{:S(2)}) collective-permute-start(f32[72,1024]{1,0:T(8,128)} %get-tuple-element.20), channel_id=1, source_target_pairs={{8,0},{16,8},{24,16},{32,24},{40,32},{48,40},{56,48},{64,56},{72,6... | collective-permute-start | bytes 884744 | tf_op jit(solution)/shard_map/ppermute | solution.py:454
  21.7 0.0 copy-start
  21.7 2.2 %copy-done = f32[16,72,1024]{2,1,0:T(8,128)} copy-done((f32[16,72,1024]{2,1,0:T(8,128)}, f32[16,72,1024]{2,1,0:T(8,128)S(1)}, u32[]{:S(2)}) %copy-start) | copy-done | bytes 4718616
  23.9 0.0 collective-permute-done.1.halo_e
  23.9 0.1 fusion
  24.0 0.0 collective-permute-done.halo_w
  24.0 0.0 copy-done.10
  24.0 0.1 fusion.1
  24.1 0.8 concatenate.9
  24.9 4.7 %collective-permute-start.4 = (f32[64,1152]{1,0:T(8,128)}, f32[64,1152]{1,0:T(8,128)}, u32[]{:S(2)}, u32[]{:S(2)}) collective-permute-start(f32[64,1152]{1,0:T(8,128)} %concatenate.9), channel_id=1, source_target_pairs={{0,8},{8,16},{16,24},{24,32},{32,40},{40,48},{48,56},{56,64},{64,7... | collective-permute-start | bytes 884744 | tf_op jit(solution)/shard_map/ppermute | solution.py:461
  29.6 0.8 concatenate.10
  30.4 1.3 %collective-permute-start.5 = (f32[64,1152]{1,0:T(8,128)}, f32[64,1152]{1,0:T(8,128)}, u32[]{:S(2)}, u32[]{:S(2)}) collective-permute-start(f32[64,1152]{1,0:T(8,128)} %concatenate.10), channel_id=1, source_target_pairs={{8,0},{16,8},{24,16},{32,24},{40,32},{48,40},{56,48},{64,56},{72,6... | collective-permute-start | bytes 884744 | tf_op jit(solution)/shard_map/ppermute | solution.py:462
  31.6 0.0 copy-done.14
  31.7 0.1 broadcast_in_dim.6.fi
  31.7 2.3 %copy-done.1 = f32[16,72,1024]{2,1,0:T(8,128)S(1)} copy-done((f32[16,72,1024]{2,1,0:T(8,128)S(1)}, f32[16,72,1024]{2,1,0:T(8,128)}, u32[]{:S(2)}) %copy-start.1) | copy-done | bytes 4718616
  34.1 0.8 copy-done.11
  34.8 9.4 %interior.1 = (f32[16,64,1024]{2,1,0:T(8,128)S(1)}, bf16[12,128,1024]{2,1,0:T(8,128)(2,1)S(1)}, bf16[12,128,1024]{2,1,0:T(8,128)(2,1)S(1)}, f32[128,256]{1,0:T(8,128)S(1)}) custom-call(s32[64,128]{1,0:T(8,128)S(1)} %broadcast_in_dim.6.fi, f32[16,72,1024]{2,1,0:T(8,128)S(1)} %copy-done.1, f32[72,128]{1,0:T(8,128)S(1)} %get-tuple-element.15.own_w, ...), custom_call_target="tpu_custom_call" | custom-call | flops 805306368 | bytes 33554432 | tf_op jit(solution)/shard_map/interior/pallas_call | solution.py:205
  44.3 0.0 copy-start.3
  44.3 1.7 %copy-done.3 = bf16[12,128,1024]{2,1,0:T(8,128)(2,1)} copy-done((bf16[12,128,1024]{2,1,0:T(8,128)(2,1)}, bf16[12,128,1024]{2,1,0:T(8,128)(2,1)S(1)}, u32[]{:S(2)}) %copy-start.3) | copy-done | bytes 3145752
  45.9 0.0 collective-permute-done.2.n1
  45.9 0.0 collective-permute-done.3.s1
  45.9 0.0 collective-permute-done.4.n2
  45.9 0.0 collective-permute-done.5.s2
  45.9 0.0 copy-done.12
  46.0 3.6 %edges.1 = (bf16[4,128,1024]{2,1,0:T(8,128)(2,1)S(1)}, bf16[4,128,1024]{2,1,0:T(8,128)(2,1)S(1)}, f32[80,128]{1,0:T(8,128)S(1)}) custom-call(s32[64,128]{1,0:T(8,128)S(1)} %broadcast_in_dim.6.fi, f32[16,72,1024]{2,1,0:T(8,128)S(1)} %copy-done.1, f32[72,128]{1,0:T(8,128)S(1)} %get-tuple-element.15.own_w, f32[72,128]{1,0:T(8,128)S(1)} %copy-done.12, ...), custom_call_target="tpu_custom_call" | custom-call | tf_op jit(solution)/shard_map/edges/pallas_call | solution.py:310
  49.5 0.0 copy-start.5
  49.6 1.0 copy-done.5
  50.5 1.0 copy-done.7
  51.5 0.0 collective-permute-start.6
  51.5 1.2 %collective-permute-done.6 = f32[40,128]{1,0:T(8,128)S(1)} collective-permute-done((f32[40,128]{1,0:T(8,128)S(1)}, f32[40,128]{1,0:T(8,128)S(1)}, u32[]{:S(2)}, u32[]{:S(2)}) %collective-permute-start.6) | collective-permute-done | bytes 20512 | tf_op jit(solution)/shard_map/ppermute | solution.py:435
  52.7 17.7 %all_to_all.10 = f32[16,40,128]{2,1,0:T(8,128)S(1)} all-to-all(f32[16,40,128]{2,1,0:T(8,128)S(1)} %broadcast_in_dim.7), channel_id=1, replica_groups=mesh['z'=8,'x'=4,'y'=4,'core'=2] {'x','y'}, dimensions={0} | all-to-all | bytes 655360 | tf_op jit(solution)/shard_map/all_to_all | solution.py:427
  70.5 18.9 %all_to_all.11 = f32[8,40,128]{2,1,0:T(8,128)S(1)} all-to-all(f32[8,40,128]{2,1,0:T(8,128)S(1)} %broadcast_in_dim.8), channel_id=1, replica_groups=mesh['z'=8,'x'=4,'y'=4,'core'=2] {'z'}, dimensions={0} | all-to-all | bytes 327680 | tf_op jit(solution)/shard_map/all_to_all | solution.py:427
  89.4 3.7 %collective-permute-start.7 = (f32[40,128]{1,0:T(8,128)S(1)}, f32[40,128]{1,0:T(8,128)S(1)}, u32[]{:S(2)}, u32[]{:S(2)}) collective-permute-start(f32[40,128]{1,0:T(8,128)S(1)} %reduce_sum.19), channel_id=1, source_target_pairs={{0,1},{1,0},{2,3},{3,2},{4,5},{5,4},{6,7},{7,6},{8,9},{9,8},{10,11... | collective-permute-start | bytes 61448 | tf_op jit(solution)/shard_map/ppermute | solution.py:438
  93.1 0.8 collective-permute-done.7
  94.0 0.0 copy-start.4
  94.0 1.9 %copy-done.4 = bf16[12,128,1024]{2,1,0:T(8,128)(2,1)S(1)} copy-done((bf16[12,128,1024]{2,1,0:T(8,128)(2,1)S(1)}, bf16[12,128,1024]{2,1,0:T(8,128)(2,1)}, u32[]{:S(2)}) %copy-start.4) | copy-done | bytes 3145752
  95.9 1.2 %copy-done.6 = bf16[4,128,1024]{2,1,0:T(8,128)(2,1)S(1)} copy-done((bf16[4,128,1024]{2,1,0:T(8,128)(2,1)S(1)}, bf16[4,128,1024]{2,1,0:T(8,128)(2,1)}, u32[]{:S(2)}) %copy-start.6) | copy-done | bytes 1048600
  97.1 1.2 %copy-done.8 = bf16[4,128,1024]{2,1,0:T(8,128)(2,1)S(1)} copy-done((bf16[4,128,1024]{2,1,0:T(8,128)(2,1)S(1)}, bf16[4,128,1024]{2,1,0:T(8,128)(2,1)}, u32[]{:S(2)}) %copy-start.8) | copy-done | bytes 1048600
  98.3 12.8 %basis.1 = (f32[128,16,1024]{2,1,0:T(8,128)}, f32[128,128]{1,0:T(8,128)}) custom-call(f32[80,128]{1,0:T(8,128)S(1)} %pad_maximum_fusion.refs_0_, bf16[12,128,1024]{2,1,0:T(8,128)(2,1)S(1)} %get-tuple-element.22.refs_1_, bf16[12,128,1024]{2,1,0:T(8,128)(2,1)S(1)} %copy-done.4, bf16[4,128,1024]{2,1,0:T(8,128)(2,1)S(1)} %copy-done.6, ...), custom_call_target="tpu_custom_call" | custom-call | tf_op jit(solution)/shard_map/basis/pallas_call | solution.py:406
  (19 shorter events, 0.2 us)
Async XLA Ops:
  0.6 2.2 %copy-start.2 = (f32[64,16,1024]{2,1,0:T(8,128)S(1)}, f32[64,16,1024]{2,1,0:T(8,128)}, u32[]{:S(2)}) copy-start(f32[64,16,1024]{2,1,0:T(8,128)} %u.1) | copy-start | bytes 12582916
  2.8 0.9 copy-start.9
  3.8 0.8 copy-start.13
  4.6 27.0 %copy-start.14 = (s32[64]{0:T(128)S(1)}, s32[64]{0:T(128)}, u32[]{:S(2)}) copy-start(s32[64]{0:T(128)} %param.7) | copy-start | bytes 772
  10.7 13.3 %copy-start.10 = (f32[72,128]{1,0:T(8,128)}, f32[72,128]{1,0:T(8,128)S(1)}, u32[]{:S(2)}) copy-start(f32[72,128]{1,0:T(8,128)S(1)} %get-tuple-element.16.own_e) | copy-start | bytes 110596
  10.7 13.3 %collective-permute-start = (f32[72,128]{1,0:T(8,128)S(1)}, f32[72,128]{1,0:T(8,128)S(1)}, u32[]{:S(2)}, u32[]{:S(2)}) collective-permute-start(f32[72,128]{1,0:T(8,128)S(1)} %get-tuple-element.16.own_e), channel_id=1, source_target_pairs={{0,1},{1,2},{2,3},{3,4},{4,5},{5,6},{6,7},{8,9},{9,10},{10,11},{11... | collective-permute-start | bytes 110600 | tf_op jit(solution)/shard_map/ppermute | solution.py:451
  15.3 8.6 %collective-permute-start.1 = (f32[72,128]{1,0:T(8,128)S(1)}, f32[72,128]{1,0:T(8,128)S(1)}, u32[]{:S(2)}, u32[]{:S(2)}) collective-permute-start(f32[72,128]{1,0:T(8,128)S(1)} %get-tuple-element.15.own_w), channel_id=1, source_target_pairs={{1,0},{2,1},{3,2},{4,3},{5,4},{6,5},{7,6},{9,8},{10,9},{11,10},{12... | collective-permute-start | bytes 110600 | tf_op jit(solution)/shard_map/ppermute | solution.py:452
  17.2 28.7 %collective-permute-start.2 = (f32[72,1024]{1,0:T(8,128)}, f32[72,1024]{1,0:T(8,128)S(1)}, u32[]{:S(2)}, u32[]{:S(2)}) collective-permute-start(f32[72,1024]{1,0:T(8,128)} %get-tuple-element.19), channel_id=1, source_target_pairs={{0,8},{8,16},{16,24},{24,32},{32,40},{40,48},{48,56},{56,64},{64,7... | collective-permute-start | bytes 884744 | tf_op jit(solution)/shard_map/ppermute | solution.py:453
  20.4 25.6 %collective-permute-start.3 = (f32[72,1024]{1,0:T(8,128)}, f32[72,1024]{1,0:T(8,128)}, u32[]{:S(2)}, u32[]{:S(2)}) collective-permute-start(f32[72,1024]{1,0:T(8,128)} %get-tuple-element.20), channel_id=1, source_target_pairs={{8,0},{16,8},{24,16},{32,24},{40,32},{48,40},{56,48},{64,56},{72,6... | collective-permute-start | bytes 884744 | tf_op jit(solution)/shard_map/ppermute | solution.py:454
  21.7 2.2 %copy-start = (f32[16,72,1024]{2,1,0:T(8,128)}, f32[16,72,1024]{2,1,0:T(8,128)S(1)}, u32[]{:S(2)}) copy-start(f32[16,72,1024]{2,1,0:T(8,128)S(1)} %get-tuple-element.14.uall) | copy-start | bytes 14155780
  24.9 21.1 %collective-permute-start.4 = (f32[64,1152]{1,0:T(8,128)}, f32[64,1152]{1,0:T(8,128)}, u32[]{:S(2)}, u32[]{:S(2)}) collective-permute-start(f32[64,1152]{1,0:T(8,128)} %concatenate.9), channel_id=1, source_target_pairs={{0,8},{8,16},{16,24},{24,32},{32,40},{40,48},{48,56},{56,64},{64,7... | collective-permute-start | bytes 884744 | tf_op jit(solution)/shard_map/ppermute | solution.py:461
  30.4 15.6 %collective-permute-start.5 = (f32[64,1152]{1,0:T(8,128)}, f32[64,1152]{1,0:T(8,128)}, u32[]{:S(2)}, u32[]{:S(2)}) collective-permute-start(f32[64,1152]{1,0:T(8,128)} %concatenate.10), channel_id=1, source_target_pairs={{8,0},{16,8},{24,16},{32,24},{40,32},{48,40},{56,48},{64,56},{72,6... | collective-permute-start | bytes 884744 | tf_op jit(solution)/shard_map/ppermute | solution.py:462
  31.7 2.3 %copy-start.1 = (f32[16,72,1024]{2,1,0:T(8,128)S(1)}, f32[16,72,1024]{2,1,0:T(8,128)}, u32[]{:S(2)}) copy-start(f32[16,72,1024]{2,1,0:T(8,128)} %copy-done) | copy-start | bytes 14155780
  34.1 0.8 copy-start.11
  34.8 11.1 %copy-start.12 = (f32[72,128]{1,0:T(8,128)S(1)}, f32[72,128]{1,0:T(8,128)}, u32[]{:S(2)}) copy-start(f32[72,128]{1,0:T(8,128)} %copy-done.10) | copy-start | bytes 110596
  44.3 1.7 %copy-start.3 = (bf16[12,128,1024]{2,1,0:T(8,128)(2,1)}, bf16[12,128,1024]{2,1,0:T(8,128)(2,1)S(1)}, u32[]{:S(2)}) copy-start(bf16[12,128,1024]{2,1,0:T(8,128)(2,1)S(1)} %get-tuple-element.23.refs_2_) | copy-start | bytes 9437188
  49.5 1.0 copy-start.5
  50.5 1.0 copy-start.7
  51.5 1.2 %collective-permute-start.6 = (f32[40,128]{1,0:T(8,128)S(1)}, f32[40,128]{1,0:T(8,128)S(1)}, u32[]{:S(2)}, u32[]{:S(2)}) collective-permute-start(f32[40,128]{1,0:T(8,128)S(1)} %slice_select_fusion), channel_id=1, source_target_pairs={{0,1},{1,0},{2,3},{3,2},{4,5},{5,4},{6,7},{7,6},{8,9},{9,8},{10,11... | collective-permute-start | bytes 61448 | tf_op jit(solution)/shard_map/ppermute | solution.py:435
  89.4 4.6 %collective-permute-start.7 = (f32[40,128]{1,0:T(8,128)S(1)}, f32[40,128]{1,0:T(8,128)S(1)}, u32[]{:S(2)}, u32[]{:S(2)}) collective-permute-start(f32[40,128]{1,0:T(8,128)S(1)} %reduce_sum.19), channel_id=1, source_target_pairs={{0,1},{1,0},{2,3},{3,2},{4,5},{5,4},{6,7},{7,6},{8,9},{9,8},{10,11... | collective-permute-start | bytes 61448 | tf_op jit(solution)/shard_map/ppermute | solution.py:438
  94.0 1.9 %copy-start.4 = (bf16[12,128,1024]{2,1,0:T(8,128)(2,1)S(1)}, bf16[12,128,1024]{2,1,0:T(8,128)(2,1)}, u32[]{:S(2)}) copy-start(bf16[12,128,1024]{2,1,0:T(8,128)(2,1)} %copy-done.3) | copy-start | bytes 9437188
  95.9 1.2 %copy-start.6 = (bf16[4,128,1024]{2,1,0:T(8,128)(2,1)S(1)}, bf16[4,128,1024]{2,1,0:T(8,128)(2,1)}, u32[]{:S(2)}) copy-start(bf16[4,128,1024]{2,1,0:T(8,128)(2,1)} %copy-done.5) | copy-start | bytes 3145732
  97.1 1.2 %copy-start.8 = (bf16[4,128,1024]{2,1,0:T(8,128)(2,1)S(1)}, bf16[4,128,1024]{2,1,0:T(8,128)(2,1)}, u32[]{:S(2)}) copy-start(bf16[4,128,1024]{2,1,0:T(8,128)(2,1)} %copy-done.7) | copy-start | bytes 3145732

commit v2 on v1

v2 whole, which is shorter than its diff:
```python
import math

import jax
import jax.numpy as jnp
from jax import lax
from jax.experimental import pallas as pl
from jax.experimental.pallas import tpu as pltpu
from jax.sharding import Mesh, PartitionSpec as P

F32, BF16 = jnp.float32, jnp.bfloat16
S, ROWS, COLS, FIELDS = 64, 16, 1024, 4
SNAP = 2 * S
TILES, GROUPS = COLS // 128, S // 8
EXT = S + 8
KAP, DEC = S, S + FIELDS
HALF = (S + 16) // 2
THIRD = (ROWS - 4) // 3
BLOCK = 16
ROWAXIS, COLAXIS = ("z", "x"), ("y", "core")
FIELD, MESSAGE = 2 * COLS, 2 * COLS + 128
HBM = pl.BlockSpec(memory_space=pltpu.HBM)
VM = pl.BlockSpec(memory_space=pltpu.VMEM)


def params(mib):
    return pltpu.CompilerParams(vmem_limit_bytes=mib * 2**20)


def lanes():
    return lax.broadcasted_iota(jnp.int32, (8, 128), 1)


def tile(t):
    return slice(128 * t, 128 * t + 128)


def group(g):
    return slice(8 * g, 8 * g + 8)


def odd_row_device():
    return (lax.axis_index("x") & 1) == 1


def odd_column_device():
    return lax.axis_index("core") == 1


def row_kernel(u, kap, dec, first_to, second_to, usem, ksem):
    def send(order):
        copies = []
        for h, (to, near, far) in enumerate(order):
            copies.append(pltpu.make_async_copy(u.at[:, near, :], to.at[:, 0:COLS], usem.at[h, 0]))
            copies.append(pltpu.make_async_copy(u.at[:, far, :], to.at[:, COLS : 2 * COLS], usem.at[h, 1]))
        for copy in copies:
            copy.start()
        small = []
        for h, (to, near, _) in enumerate(order):
            to[:, FIELD : FIELD + 128] = jnp.zeros((S, 128), F32)
            for t in range(TILES):
                tiles = to.at[8 * t : 8 * t + FIELDS, FIELD : FIELD + 128]
                small.append(pltpu.make_async_copy(kap.at[:, near, tile(t)], tiles, ksem.at[h, 0, t]))
                line = to.at[8 * t + FIELDS : 8 * t + FIELDS + 1, FIELD : FIELD + 128]
                small.append(pltpu.make_async_copy(dec.at[near : near + 1, tile(t)], line, ksem.at[h, 1, t]))
        for copy in small:
            copy.start()
        for copy in copies + small:
            copy.wait()

    odd = odd_row_device()
    top, bottom = (0, 1), (ROWS - 1, ROWS - 2)

    @pl.when(odd)
    def _():
        send(((first_to, *top), (second_to, *bottom)))

    @pl.when(jnp.logical_not(odd))
    def _():
        send(((first_to, *bottom), (second_to, *top)))


def rows(initial, kappa, decay):
    message = pltpu.VMEM((S, MESSAGE), F32)
    return pl.pallas_call(
        row_kernel,
        name="rows",
        in_specs=[HBM] * 3,
        out_specs=[VM] * 2,
        out_shape=[message, message],
        scratch_shapes=[pltpu.SemaphoreType.DMA((2, 2)), pltpu.SemaphoreType.DMA((2, 2, TILES))],
        compiler_params=params(58),
    )(initial, kappa, decay)


def column_kernel(u, kap, dec, uall, west, east, first_to, second_to, sems):
    for x in range(ROWS):
        uall[x, S:EXT, :] = jnp.zeros((8, COLS), F32)
    copies = []
    for x in range(ROWS):
        copies.append(
            (
                pltpu.make_async_copy(u.at[:, x, :], uall.at[x, 0:S, :], sems.at[0, x]),
                pltpu.make_async_copy(kap.at[:, x, :], uall.at[x, KAP : KAP + FIELDS, :], sems.at[1, x]),
                pltpu.make_async_copy(dec.at[x : x + 1, :], uall.at[x, DEC : DEC + 1, :], sems.at[2, x]),
            )
        )
        for copy in copies[x]:
            copy.start()
    lane = lanes()
    w = [jnp.zeros((8, 128), F32) for _ in range(GROUPS + 1)]
    e = [jnp.zeros((8, 128), F32) for _ in range(GROUPS + 1)]
    for x in range(ROWS):
        for copy in copies[x]:
            copy.wait()
        for g in range(GROUPS + 1):
            first, last = uall[x, group(g), tile(0)], uall[x, group(g), tile(TILES - 1)]
            w[g] = jnp.where(lane == x, pltpu.roll(first, x, 1), w[g])
            e[g] = jnp.where(lane == x, pltpu.roll(last, x + 1, 1), e[g])
            if g < GROUPS:
                w[g] = jnp.where(lane == ROWS + x, pltpu.roll(first, ROWS + x - 1, 1), w[g])
                e[g] = jnp.where(lane == ROWS + x, pltpu.roll(last, ROWS + x + 2, 1), e[g])
    for g in range(GROUPS + 1):
        west[group(g), :] = w[g]
        east[group(g), :] = e[g]
        odd = odd_column_device()
        first_to[group(g), :] = jnp.where(odd, w[g], e[g])
        second_to[group(g), :] = jnp.where(odd, e[g], w[g])


def columns(initial, kappa, decay):
    col = pltpu.VMEM((EXT, 128), F32)
    return pl.pallas_call(
        column_kernel,
        name="columns",
        in_specs=[HBM] * 3,
        out_specs=[VM] * 5,
        out_shape=[pltpu.VMEM((ROWS, EXT, COLS), F32), col, col, col, col],
        scratch_shapes=[pltpu.SemaphoreType.DMA((3, ROWS))],
        compiler_params=params(54),
    )(initial, kappa, decay)


def corner_kernel(first_from, second_from, halo_w, halo_e, first_to, second_to):
    lane = lanes()
    odd, odd_row = odd_column_device(), odd_row_device()
    for g in range(GROUPS + 1):
        a, b = first_from[group(g), :], second_from[group(g), :]
        w, e = jnp.where(odd, a, b), jnp.where(odd, b, a)
        halo_w[group(g), :] = w
        halo_e[group(g), :] = e
        if g < GROUPS:
            top = jnp.where(lane == 0, w, pltpu.roll(e, 1, 1))
            w, e = pltpu.roll(w, 128 - (ROWS - 1), 1), pltpu.roll(e, 128 - (ROWS - 2), 1)
            bottom = jnp.where(lane == 0, w, e)
            first_to[group(g), :] = jnp.where(odd_row, top, bottom)
            second_to[group(g), :] = jnp.where(odd_row, bottom, top)


def corners(first_from, second_from):
    halo, message = pltpu.VMEM((EXT, 128), F32), pltpu.VMEM((S, 128), F32)
    return pl.pallas_call(
        corner_kernel,
        name="corners",
        in_specs=[VM] * 2,
        out_specs=[VM] * 4,
        out_shape=[halo, halo, message, message],
        compiler_params=params(2),
    )(first_from, second_from)


def fields(k):
    b = k * 0.2
    keep = 1.0 - jnp.broadcast_to(k[FIELDS : FIELDS + 1, :], (8, 128))
    return keep - 4.0 * b, b


def choose(k, f):
    return jnp.take_along_axis(k, f, axis=0, mode="promise_in_bounds")


def step_row(fi, load_field, center, above, below, edge_w, edge_e, emit):
    lane = lanes()
    low, high = lane == 0, lane == 127
    from_w = [edge_w(g) for g in range(GROUPS)]
    from_e = [pltpu.roll(center(g, 0), 127, 1) for g in range(GROUPS)]
    for t in range(TILES):
        ka, kb = fields(load_field(t))
        held = None
        for g in range(GROUPS):
            here = center(g, t)
            right = pltpu.roll(here, 1, 1)
            west = jnp.where(low, from_w[g], right)
            from_w[g] = right
            nxt = pltpu.roll(center(g, t + 1), 127, 1) if t + 1 < TILES else edge_e(g)
            east = jnp.where(high, nxt, from_e[g])
            from_e[g] = nxt
            a, b = choose(ka, fi[group(g), :]), choose(kb, fi[group(g), :])
            new = a * here + b * ((above(g, t) + below(g, t)) + (west + east))
            if g % 2 == 0:
                held = new
            else:
                emit(g - 1, t, held, new)


def split_store(ref, index, g, t, first, second):
    both = jnp.concatenate([first, second], 0)
    top = both.astype(BF16)
    ref[index, 8 * g : 8 * g + 16, tile(t)] = top
    ref[index, S + 8 * g : S + 8 * g + 16, tile(t)] = (both - top.astype(F32)).astype(BF16)


def gram(acc, f, s):
    hi = jnp.concatenate([f[:S, :], s[:S, :]], 0)
    rhs = jnp.concatenate([hi, f[S:, :], s[S:, :]], 0)
    acc[...] += lax.dot_general(hi, rhs, (((1,), (1,)), ((), ())), preferred_element_type=F32)


def column_step(fi, halo, own, g, up=None, down=None):
    lane = lanes()
    one = halo[group(g), :]
    two = pltpu.roll(one, 128 - ROWS, 1)
    ka, kb = fields(halo[S:EXT, :])
    a, b = choose(ka, fi[group(g), :]), choose(kb, fi[group(g), :])
    above, below = pltpu.roll(one, 1, 1), pltpu.roll(one, 127, 1)
    if up is not None:
        above = jnp.where(lane == 0, up, above)
        below = jnp.where(lane == ROWS - 1, down, below)
    return a * one + b * ((above + below) + (two + own[group(g), :]))


def interior_kernel(fi, uall, own_w, own_e, halo_w, halo_e, first, f0, f1, f2, s0, s1, s2, acc, col_w, col_e):
    acc[...] = jnp.zeros_like(acc)
    for g in range(GROUPS):
        col_w[group(g), :] = column_step(fi, halo_w, own_w, g)
        col_e[group(g), :] = column_step(fi, halo_e, own_e, g)

    def field(x):
        return lambda t: uall[x, S:EXT, tile(t)]

    def one(x, ref=None, index=None):
        def emit(g, t, p, q):
            first[x, group(g), tile(t)] = p
            first[x, group(g + 1), tile(t)] = q
            if ref is not None:
                split_store(ref, index, g, t, p, q)

        step_row(
            fi,
            field(x),
            lambda g, t: uall[x, group(g), tile(t)],
            lambda g, t: uall[x - 1, group(g), tile(t)],
            lambda g, t: uall[x + 1, group(g), tile(t)],
            lambda g: pltpu.roll(halo_w[group(g), :], (128 - x) % 128, 1),
            lambda g: pltpu.roll(halo_e[group(g), :], 127 - x, 1),
            emit,
        )

    def two(x, ref, index):
        step_row(
            fi,
            field(x),
            lambda g, t: first[x, group(g), tile(t)],
            lambda g, t: first[x - 1, group(g), tile(t)],
            lambda g, t: first[x + 1, group(g), tile(t)],
            lambda g: pltpu.roll(col_w[group(g), :], (128 - x) % 128, 1),
            lambda g: pltpu.roll(col_e[group(g), :], 127 - x, 1),
            lambda g, t, p, q: split_store(ref, index, g, t, p, q),
        )

    one(1)
    one(2, f0, 0)
    one(3, f1, 0)
    two(2, s0, 0)

    def body(i, carry):
        x = 4 + 3 * i
        gram(acc, f0[i], s0[i])
        one(x, f2, i)
        two(x - 1, s1, i)
        gram(acc, f1[i], s1[i])
        one(x + 1, f0, i + 1)
        two(x, s2, i)
        gram(acc, f2[i], s2[i])
        one(x + 2, f1, i + 1)
        two(x + 1, s0, i + 1)
        return carry

    lax.fori_loop(0, THIRD - 1, body, 0)
    end = THIRD - 1
    gram(acc, f0[end], s0[end])
    one(ROWS - 3, f2, end)
    two(ROWS - 4, s1, end)
    gram(acc, f1[end], s1[end])
    one(ROWS - 2)
    two(ROWS - 3, s2, end)
    gram(acc, f2[end], s2[end])


def interior(fi, uall, own_w, own_e, halo_w, halo_e):
    snap = pltpu.VMEM((THIRD, SNAP, COLS), BF16)
    return pl.pallas_call(
        interior_kernel,
        name="interior",
        in_specs=[VM] * 6,
        out_specs=[VM] * 8,
        out_shape=[pltpu.VMEM((ROWS, S, COLS), F32), *[snap] * 6, pltpu.VMEM((SNAP, 2 * SNAP), F32)],
        scratch_shapes=[pltpu.VMEM((S, 128), F32)] * 2,
        cost_estimate=pl.CostEstimate(flops=2 * 12 * SNAP * 2 * SNAP * COLS, bytes_accessed=2**25, transcendentals=0),
        compiler_params=params(8),
    )(fi, uall, own_w, own_e, halo_w, halo_e)


def edge_kernel(
    fi, uall, own_w, own_e, halo_w, halo_e, first, inner, n1, s1, nc, sc, snap_f, snap_s, keep, give, col_w, col_e, edge, acc, packed
):
    acc[...] = inner[...]
    odd = odd_row_device()
    for g in range(GROUPS):
        a, b = nc[group(g), :], sc[group(g), :]
        up, down = jnp.where(odd, a, b), jnp.where(odd, b, a)
        col_w[group(g), :] = column_step(fi, halo_w, own_w, g, up, pltpu.roll(down, ROWS - 1, 1))
        col_e[group(g), :] = column_step(fi, halo_e, own_e, g, pltpu.roll(up, 127, 1), pltpu.roll(down, ROWS - 2, 1))

    def rows(ref, base):
        return lambda g, t: ref[group(g), base + 128 * t : base + 128 * t + 128]

    def at(ref, x):
        return lambda g, t: ref[x, group(g), tile(t)]

    def field(x):
        return lambda t: uall[x, S:EXT, tile(t)]

    def pick(ref, x, to):
        return lambda g: pltpu.roll(ref[group(g), :], (to + 128 - x) & 127, 1)

    for near, corner, at_top in ((n1, nc, odd), (s1, sc, jnp.logical_not(odd))):
        row, inside, deeper = (jnp.where(at_top, i, ROWS - 1 - i) for i in range(3))

        def put(index):
            def emit(g, t, p, q):
                edge[index, group(g), tile(t)] = p
                edge[index, group(g + 1), tile(t)] = q

            return emit

        def put_both(index, target):
            def emit(g, t, p, q):
                put(index)(g, t, p, q)
                split_store(snap_f, target, g, t, p, q)

            return emit

        def put_second(target):
            return lambda g, t, p, q: split_store(snap_s, target, g, t, p, q)

        outer, inner_slot = jnp.where(at_top, 0, 3), jnp.where(at_top, 1, 2)
        step_row(
            fi,
            lambda t, near=near: near[8 * t : 8 * t + 8, FIELD : FIELD + 128],
            rows(near, 0),
            rows(near, COLS),
            at(uall, row),
            pick(corner, 0, 0),
            pick(corner, 1, 127),
            put(0),
        )
        step_row(
            fi, field(row), at(uall, row), rows(near, 0), at(uall, inside),
            pick(halo_w, row, 0), pick(halo_e, row, 127), put_both(1, outer),
        )
        step_row(
            fi, field(row), at(edge, 1), at(edge, 0), at(first, inside),
            pick(col_w, row, 0), pick(col_e, row, 127), put_second(outer),
        )
        step_row(
            fi, field(inside), at(first, inside), at(edge, 1), at(first, deeper),
            pick(col_w, inside, 0), pick(col_e, inside, 127), put_second(inner_slot),
        )
        for t in range(TILES):
            for g in range(0, GROUPS, 2):
                split_store(
                    snap_f, inner_slot, g, t,
                    first[inside, group(g), tile(t)], first[inside, group(g + 1), tile(t)],
                )
        gram(acc, snap_f[outer], snap_s[outer])
        gram(acc, snap_f[inner_slot], snap_s[inner_slot])
    cross = acc[:, SNAP:]
    full = acc[:, :SNAP] + (cross + cross.T)
    top, bottom = full[:S, :], pltpu.roll(full[S:, :], S, 1)
    r = lax.broadcasted_iota(jnp.int32, (S, SNAP), 0)
    c = lax.broadcasted_iota(jnp.int32, (S, SNAP), 1)
    packed[0:S, :] = jnp.where((c < S) & (r > c), bottom, top)
    diag = jnp.sum(jnp.where(r == c, bottom, 0.0), axis=0, keepdims=True)
    packed[S : S + 8, :] = jnp.where(lax.broadcasted_iota(jnp.int32, (8, SNAP), 0) == 0, diag, 0.0)
    packed[S + 8 :, :] = jnp.zeros((8, SNAP), F32)
    second = lax.axis_index("core") == 1
    a, b = packed[:HALF, :], packed[HALF:, :]
    keep[...] = jnp.where(second, b, a)
    give[...] = jnp.where(second, a, b)


def edges(fi, uall, own_w, own_e, halo_w, halo_e, first, inner, n1, s1, nc, sc):
    snap, half = pltpu.VMEM((4, SNAP, COLS), BF16), pltpu.VMEM((HALF, SNAP), F32)
    return pl.pallas_call(
        edge_kernel,
        name="edges",
        in_specs=[VM] * 12,
        out_specs=[VM] * 4,
        out_shape=[snap, snap, half, half],
        scratch_shapes=[
            pltpu.VMEM((S, 128), F32),
            pltpu.VMEM((S, 128), F32),
            pltpu.VMEM((2, S, COLS), F32),
            pltpu.VMEM((SNAP, 2 * SNAP), F32),
            pltpu.VMEM((2 * HALF, SNAP), F32),
        ],
        compiler_params=params(8),
    )(fi, uall, own_w, own_e, halo_w, halo_e, first, inner, n1, s1, nc, sc)


def unpack(packed):
    top, diag = packed[0:S, :], packed[S : S + 1, :]
    r = lax.broadcasted_iota(jnp.int32, (S, SNAP), 0)
    c = lax.broadcasted_iota(jnp.int32, (S, SNAP), 1)
    upper = jnp.where(r <= c, top, 0.0)
    lower = pltpu.roll(jnp.where((r > c) & (c < S), top, 0.0), S, 1)
    on_diag = jnp.where(r == c - S, pltpu.roll(jnp.broadcast_to(diag, (8, SNAP)), S, 1)[0:1, :], 0.0)
    zero = jnp.zeros_like(lower)
    return jnp.concatenate([upper, on_diag], 0) + jnp.concatenate([zero, lower], 0).T


def factor(m, z):
    sub = lax.broadcasted_iota(jnp.int32, (8, 128), 0)
    for k in range(SNAP // BLOCK):
        lo = k * BLOCK
        panel = m[lo : lo + BLOCK, :]
        p = {}
        for i in range(BLOCK):
            for j in range(i, BLOCK):
                p[i, j] = jnp.broadcast_to(panel[i : i + 1, lo + j : lo + j + 1], (8, 128))
        rows = [[jnp.broadcast_to(panel[i : i + 1, tile(h)], (8, 128)) for h in range(2)] for i in range(BLOCK)]
        for j in range(BLOCK):
            r = lax.rsqrt(p[j, j])
            u = {i: p[j, i] * r for i in range(j + 1, BLOCK)}
            for i in range(j + 1, BLOCK):
                for l in range(i, BLOCK):
                    p[i, l] = p[i, l] - u[i] * u[l]
            rows[j] = [v * r for v in rows[j]]
            for i in range(j + 1, BLOCK):
                rows[i] = [v - u[i] * w for v, w in zip(rows[i], rows[j])]
        for part in range(BLOCK // 8):
            for h in range(2):
                v = rows[8 * part][h]
                for i in range(1, 8):
                    v = jnp.where(sub == i, rows[8 * part + i][h], v)
                z[lo + 8 * part : lo + 8 * part + 8, tile(h)] = v
        if lo + BLOCK < SNAP:
            done = z[lo : lo + BLOCK, :]
            update = lax.dot_general(
                done[:, :SNAP], done, (((0,), (0,)), ((), ())),
                precision=lax.Precision.HIGHEST, preferred_element_type=F32,
            )
            m[lo + BLOCK :, :] = m[lo + BLOCK :, :] - update[lo + BLOCK :, :]


def basis_kernel(scale, mine, other, *refs):
    (*snaps, out, tri, m, z, buf, sems) = refs
    r = lax.broadcasted_iota(jnp.int32, (SNAP, SNAP), 0)
    c = lax.broadcasted_iota(jnp.int32, (SNAP, SNAP), 1)
    second = lax.axis_index("core") == 1
    a, b = mine[...], other[...]
    m[:, :SNAP] = unpack(jnp.concatenate([jnp.where(second, b, a), jnp.where(second, a, b)], 0))
    m[:, SNAP:] = jnp.where(r == c, 1.0, 0.0)
    factor(m, z)
    tri[...] = jnp.where(r <= c, z[:, :SNAP], 0.0) * (1.0 / scale)
    w = jnp.where(r >= c, z[:, SNAP:], 0.0) * scale
    top = w.astype(BF16)
    rest = (w - top.astype(F32)).astype(BF16)
    twice = jnp.concatenate([top, top], 1)

    def copy(x):
        return pltpu.make_async_copy(buf.at[x], out.at[:, x, :], sems.at[x])

    def row(x, f, s):
        hi = jnp.concatenate([f[:S, :], s[:S, :]], 0)
        both = jnp.concatenate([hi, f[S:, :], s[S:, :]], 0)
        buf[x] = jnp.dot(twice, both, preferred_element_type=F32) + jnp.dot(rest, hi, preferred_element_type=F32)
        copy(x).start()

    def body(i, carry):
        for k in range(3):
            row(2 + 3 * i + k, snaps[k][i], snaps[3 + k][i])
        return carry

    lax.fori_loop(0, THIRD, body, 0)
    for i, x in enumerate((0, 1, ROWS - 2, ROWS - 1)):
        row(x, snaps[6][i], snaps[7][i])
    for x in range(ROWS):
        copy(x).wait()


def make_basis(scale, mine, other, *snaps):
    def kernel(*refs):
        basis_kernel(scale, *refs)

    return pl.pallas_call(
        kernel,
        name="basis",
        in_specs=[VM] * 10,
        out_specs=[HBM, VM],
        out_shape=[
            jax.ShapeDtypeStruct((SNAP, ROWS, COLS), F32),
            jax.ShapeDtypeStruct((SNAP, SNAP), F32),
        ],
        scratch_shapes=[
            pltpu.VMEM((SNAP, 2 * SNAP), F32),
            pltpu.VMEM((SNAP, 2 * SNAP), F32),
            pltpu.VMEM((ROWS, SNAP, COLS), F32),
            pltpu.SemaphoreType.DMA((ROWS,)),
        ],
        compiler_params=params(16),
    )(mine, other, *snaps)


def spread_sum(value, axis):
    count = lax.axis_size(axis)
    every = lax.all_to_all(jnp.broadcast_to(value[None], (count, *value.shape)), axis, 0, 0)
    parts = [every[i] for i in range(count)]
    while len(parts) > 1:
        parts = [a + b for a, b in zip(parts[::2], parts[1::2], strict=True)]
    return parts[0]


def pairs(axis, start):
    lower = range(start, lax.axis_size(axis) - 1, 2)
    return [(i, i + 1) for i in lower] + [(i + 1, i) for i in lower]


def shards(initial, kappa, decay, field_index):
    fi = jnp.broadcast_to(field_index[:, None], (S, 128))
    row_a, row_b = rows(initial, kappa, decay)
    near_a, near_b = lax.ppermute(row_a, ROWAXIS, pairs(ROWAXIS, 0)), lax.ppermute(row_b, ROWAXIS, pairs(ROWAXIS, 1))
    uall, own_w, own_e, col_a, col_b = columns(initial, kappa, decay)
    col_a, col_b = lax.ppermute(col_a, COLAXIS, pairs(COLAXIS, 0)), lax.ppermute(col_b, COLAXIS, pairs(COLAXIS, 1))
    halo_w, halo_e, corner_a, corner_b = corners(col_a, col_b)
    corner_a = lax.ppermute(corner_a, ROWAXIS, pairs(ROWAXIS, 0))
    corner_b = lax.ppermute(corner_b, ROWAXIS, pairs(ROWAXIS, 1))
    first, *inner_snaps, inner = interior(fi, uall, own_w, own_e, halo_w, halo_e)
    edge_f, edge_s, keep, give = edges(
        fi, uall, own_w, own_e, halo_w, halo_e, first, inner, near_a, near_b, corner_a, corner_b
    )
    swap = [(0, 1), (1, 0)]
    mine = keep + lax.ppermute(give, "core", swap)
    mine = spread_sum(spread_sum(mine, ("x", "y")), "z")
    other = lax.ppermute(mine, "core", swap)
    cells = lax.axis_size(ROWAXIS) * lax.axis_size(COLAXIS) * ROWS * COLS
    return make_basis(math.sqrt(cells), mine, other, *inner_snaps, edge_f, edge_s)


def solution(mesh):
    wide, narrow = mesh.devices.shape
    fine = Mesh(mesh.devices.reshape(wide // 4, 4, narrow // 2, 2), ("z", "x", "y", "core"))
    grid = P(None, ROWAXIS, COLAXIS)
    return jax.shard_map(
        shards,
        mesh=fine,
        in_specs=(grid, grid, P(ROWAXIS, COLAXIS), P()),
        out_specs=(grid, P()),
        check_vma=False,
    )
```

time: 112 us -> 78.8 us (0.70)
  local copies, waits for them, and re-layouts: 19.1 us -> 0.11 us
  Pallas kernels: 31.8 us -> 25.2 us
  starting transfers between devices: 20.7 us -> 14.7 us
  blocking collectives: 36.6 us -> 32.9 us
  waiting for transfers between devices: 2.04 us -> 4.75 us
    unnamed x30 -> x2, local copies, waits for them, and re-layouts: 17.2 us -> 0.01 us
    ppermute x8, starting transfers between devices: 20.7 us -> 14.7 us  [the longest x1 3.54 us: shards(): other = lax.ppermute(mine, 'core', swap)]
    pallas_call x1, Pallas kernels: 9.4 us -> 5.38 us  [interior(): pl.pallas_call(interior_kernel, name='interior', in_specs=[VM] * 6, out_s...]
    all_to_all x2, blocking collectives: 36.6 us -> 32.9 us  [spread_sum(): lax.all_to_all(jnp.broadcast_to(value[None], (count, *value.shape)), axis...]
    ppermute x8, waiting for transfers between devices: 2.04 us -> 4.75 us  [the longest x1 2.71 us: shards(): lax.ppermute(col_b, COLAXIS, pairs(COLAXIS, 1))]
    concatenate x2 -> x0, local copies, waits for them, and re-layouts: 1.59 us -> none  [far(): return jnp.concatenate([uall[row, :S, :], *ends, pad], 1)]
    pallas_call x1, Pallas kernels: 3.59 us -> 2.23 us  [edges(): pl.pallas_call(edge_kernel, name='edges', in_specs=[VM] * 12, out_specs=[...]
    pallas_call x2 -> x4, Pallas kernels: 18.9 us -> 17.6 us  [the longest x1 12.6 us: make_basis(): pl.pallas_call(kernel, name='basis', in_specs=[VM] * 10, out_specs=[HBM,...]
  transfers between devices with their start and end apart: 8 -> 8, of which waited for: 2 -> 3; matrix products, arithmetic and copies ran while one was open for 2% -> 0% of each run, Pallas kernels for 8% -> 11%
where the time goes in v2:
time: 78.8 us; the launch traced here: 78.6 us
  blocking collectives  32.9 us (42%)
  Pallas kernels  25.2 us (32%)
  starting transfers between devices  14.7 us (19%)
  waiting for transfers between devices  4.75 us (6%)
  between operations  0.94 us (1%)
    all_to_all x2, blocking collectives, spread_sum(): lax.all_to_all(jnp.broadcast_to(value[None], (count, *value.shape)), axis...  32.9 us
    pallas_call x1, Pallas kernels, make_basis(): pl.pallas_call(kernel, name='basis', in_specs=[VM] * 10, out_specs=[HBM,...  12.6 us
    pallas_call x1, Pallas kernels, interior(): pl.pallas_call(interior_kernel, name='interior', in_specs=[VM] * 6, out_s...  5.38 us
    ppermute x1, starting transfers between devices, shards(): other = lax.ppermute(mine, 'core', swap)  3.54 us
    ppermute x1, starting transfers between devices, shards(): corner_a = lax.ppermute(corner_a, ROWAXIS, pairs(ROWAXIS, 0))  3.43 us
    pallas_call x1, Pallas kernels, columns(): pl.pallas_call(column_kernel, name='columns', in_specs=[HBM] * 3, out_spe...  3.21 us
    ppermute x1, starting transfers between devices, shards(): lax.ppermute(col_b, COLAXIS, pairs(COLAXIS, 1))  2.83 us
    ppermute x1, waiting for transfers between devices, shards(): lax.ppermute(col_b, COLAXIS, pairs(COLAXIS, 1))  2.71 us
  transfers between devices with their start and end apart: 8, of which 3 were waited for; matrix products, arithmetic and copies ran while one was open for 0% of the time, Pallas kernels for 11%

profile of v2, /device:TPU:1, one launch (start us, length us, event | category | flops | bytes accessed | tf_op | source)
XLA Modules:
  0.0 78.6 jit_solution(8532172011464481226)
XLA Ops:
  0.6 0.0 copy-start
  0.6 1.7 %rows.1 = (f32[64,2176]{1,0:T(8,128)S(1)}, f32[64,2176]{1,0:T(8,128)S(1)}) custom-call(f32[64,16,1024]{2,1,0:T(8,128)} %u.3, f32[4,16,1024]{2,1,0:T(8,128)} %kap.3, f32[16,1024]{1,0:T(8,128)} %dec.3), custom_call_target="tpu_custom_call" | custom-call | tf_op jit(solution)/shard_map/rows/pallas_call | solution.py:84
  2.3 2.1 %collective-permute-start.2 = (f32[64,2176]{1,0:T(8,128)S(1)}, f32[64,2176]{1,0:T(8,128)S(1)}, u32[]{:S(2)}, u32[]{:S(2)}) collective-permute-start(f32[64,2176]{1,0:T(8,128)S(1)} %get-tuple-element.34), channel_id=1, source_target_pairs={{0,8},{16,24},{32,40},{48,56},{64,72},{80,88},{96,104},{112,120},{... | collective-permute-start | bytes 1671176 | tf_op jit(solution)/shard_map/ppermute | solution.py:542
  4.4 0.7 collective-permute-start.3
  5.1 3.2 %columns.1 = (f32[16,72,1024]{2,1,0:T(8,128)S(1)}, f32[72,128]{1,0:T(8,128)S(1)}, f32[72,128]{1,0:T(8,128)S(1)}, f32[72,128]{1,0:T(8,128)S(1)}, f32[72,128]{1,0:T(8,128)S(1)}) custom-call(f32[64,16,1024]{2,1,0:T(8,128)} %u.3, f32[4,16,1024]{2,1,0:T(8,128)} %kap.3, f32[16,1024]{1,0:T(8,128)} %dec.3), custom_call_target="tpu_custom_call" | custom-call | tf_op jit(solution)/shard_map/columns/pallas_call | solution.py:132
  8.4 1.3 %collective-permute-start = (f32[72,128]{1,0:T(8,128)S(1)}, f32[72,128]{1,0:T(8,128)S(1)}, u32[]{:S(2)}, u32[]{:S(2)}) collective-permute-start(f32[72,128]{1,0:T(8,128)S(1)} %get-tuple-element.28), channel_id=1, source_target_pairs={{0,1},{2,3},{4,5},{6,7},{1,0},{3,2},{5,4},{7,6},{8,9},{10,11},{12,... | collective-permute-start | bytes 110600 | tf_op jit(solution)/shard_map/ppermute | solution.py:544
  9.7 2.8 %collective-permute-start.1 = (f32[72,128]{1,0:T(8,128)S(1)}, f32[72,128]{1,0:T(8,128)S(1)}, u32[]{:S(2)}, u32[]{:S(2)}) collective-permute-start(f32[72,128]{1,0:T(8,128)S(1)} %get-tuple-element.29), channel_id=1, source_target_pairs={{1,2},{3,4},{5,6},{2,1},{4,3},{6,5},{9,10},{11,12},{13,14},{10,9},... | collective-permute-start | bytes 110600 | tf_op jit(solution)/shard_map/ppermute | solution.py:544
  12.5 0.0 collective-permute-done.first_from
  12.5 2.7 %collective-permute-done.1.second_from = f32[72,128]{1,0:T(8,128)S(1)} collective-permute-done((f32[72,128]{1,0:T(8,128)S(1)}, f32[72,128]{1,0:T(8,128)S(1)}, u32[]{:S(2)}, u32[]{:S(2)}) %collective-permute-start.1) | collective-permute-done | bytes 36896 | tf_op jit(solution)/shard_map/ppermute | solution.py:544
  15.2 0.1 corners.1
  15.3 3.4 %collective-permute-start.4 = (f32[64,128]{1,0:T(8,128)S(1)}, f32[64,128]{1,0:T(8,128)S(1)}, u32[]{:S(2)}, u32[]{:S(2)}) collective-permute-start(f32[64,128]{1,0:T(8,128)S(1)} %get-tuple-element.36), channel_id=1, source_target_pairs={{0,8},{16,24},{32,40},{48,56},{64,72},{80,88},{96,104},{112,120},{... | collective-permute-start | bytes 98312 | tf_op jit(solution)/shard_map/ppermute | solution.py:546
  18.8 0.7 collective-permute-start.5
  19.4 0.0 copy-done
  19.4 0.1 broadcast_in_dim.8.fi
  19.5 5.4 %interior.1 = (f32[16,64,1024]{2,1,0:T(8,128)S(1)}, bf16[4,128,1024]{2,1,0:T(8,128)(2,1)S(1)}, bf16[4,128,1024]{2,1,0:T(8,128)(2,1)S(1)}, bf16[4,128,1024]{2,1,0...) custom-call(s32[64,128]{1,0:T(8,128)S(1)} %broadcast_in_dim.8.fi, ...), custom_call_target="tpu_custom_call" | custom-call | flops 805306368 | bytes 33554432 | tf_op jit(solution)/shard_map/interior/pallas_call | solution.py:301
  24.9 0.0 collective-permute-done.4.nc
  24.9 0.0 collective-permute-done.5.sc
  24.9 0.0 collective-permute-done.2.n1
  24.9 0.0 collective-permute-done.3.s1
  24.9 2.2 %edges.1 = (bf16[4,128,1024]{2,1,0:T(8,128)(2,1)S(1)}, bf16[4,128,1024]{2,1,0:T(8,128)(2,1)S(1)}, f32[40,128]{1,0:T(8,128)S(1)}, f32[40,128]{1,0:T(8,128)S(1)}) custom-call(s32[64,128]{1,0:T(8,128)S(1)} %broadcast_in_dim.8.fi, f32[16,72,1024]{2,1,0:T(8,128)S(1)} %get-tuple-element.25.uall, f32[72,128]{1,0:T(8,128)S(1)} %get-tuple-element.26.own_w, ...), custom_call_target="tpu_custom_call" | custom-call | tf_op jit(solution)/shard_map/edges/pallas_call | solution.py:404
  27.2 0.1 collective-permute-start.6
  27.3 1.2 %collective-permute-done.6 = f32[40,128]{1,0:T(8,128)S(1)} collective-permute-done((f32[40,128]{1,0:T(8,128)S(1)}, f32[40,128]{1,0:T(8,128)S(1)}, u32[]{:S(2)}, u32[]{:S(2)}) %collective-permute-start.6) | collective-permute-done | bytes 20512 | tf_op jit(solution)/shard_map/ppermute | solution.py:553
  28.5 17.1 %all_to_all.10 = f32[16,40,128]{2,1,0:T(8,128)S(1)} all-to-all(f32[16,40,128]{2,1,0:T(8,128)S(1)} %broadcast_in_dim.9), channel_id=1, replica_groups=mesh['z'=8,'x'=4,'y'=4,'core'=2] {'x','y'}, dimensions={0} | all-to-all | bytes 655360 | tf_op jit(solution)/shard_map/all_to_all | solution.py:527
  45.6 15.8 %all_to_all.11 = f32[8,40,128]{2,1,0:T(8,128)S(1)} all-to-all(f32[8,40,128]{2,1,0:T(8,128)S(1)} %broadcast_in_dim.11), channel_id=1, replica_groups=mesh['z'=8,'x'=4,'y'=4,'core'=2] {'z'}, dimensions={0} | all-to-all | bytes 327680 | tf_op jit(solution)/shard_map/all_to_all | solution.py:527
  61.4 3.5 %collective-permute-start.7 = (f32[40,128]{1,0:T(8,128)S(1)}, f32[40,128]{1,0:T(8,128)S(1)}, u32[]{:S(2)}, u32[]{:S(2)}) collective-permute-start(f32[40,128]{1,0:T(8,128)S(1)} %fusion.2.refs_0_), channel_id=1, source_target_pairs={{0,1},{1,0},{2,3},{3,2},{4,5},{5,4},{6,7},{7,6},{8,9},{9,8},{10,11... | collective-permute-start | bytes 61448 | tf_op jit(solution)/shard_map/ppermute | solution.py:555
  65.0 0.8 %collective-permute-done.7.refs_1_ = f32[40,128]{1,0:T(8,128)S(1)} collective-permute-done((f32[40,128]{1,0:T(8,128)S(1)}, f32[40,128]{1,0:T(8,128)S(1)}, u32[]{:S(2)}, u32[]{:S(2)}) %collective-permute-start.7) | collective-permute-done | bytes 20512 | tf_op jit(solution)/shard_map/ppermute | solution.py:555
  65.8 12.6 %basis.1 = (f32[128,16,1024]{2,1,0:T(8,128)}, f32[128,128]{1,0:T(8,128)}) custom-call(f32[40,128]{1,0:T(8,128)S(1)} %fusion.2.refs_0_, f32[40,128]{1,0:T(8,128)S(1)} %collective-permute-done.7.refs_1_, bf16[4,128,1024]{2,1,0:T(8,128)(2,1)S(1)} %get-tuple-element.40.refs_2_, bf16[4,128,1024]{2,1,0:T(8,128)(2,1)S(1)} %get-tuple-element.41.refs_3_, ...), custom_call_target="tpu_custom_call" | custom-call | tf_op jit(solution)/shard_map/basis/pallas_call | solution.py:506
  (5 shorter events, 0.1 us)
Async XLA Ops:
  0.6 18.8 %copy-start = (s32[64]{0:T(128)S(1)}, s32[64]{0:T(128)}, u32[]{:S(2)}) copy-start(s32[64]{0:T(128)} %param.7) | copy-start | bytes 772
  2.3 22.6 %collective-permute-start.2 = (f32[64,2176]{1,0:T(8,128)S(1)}, f32[64,2176]{1,0:T(8,128)S(1)}, u32[]{:S(2)}, u32[]{:S(2)}) collective-permute-start(f32[64,2176]{1,0:T(8,128)S(1)} %get-tuple-element.34), channel_id=1, source_target_pairs={{0,8},{16,24},{32,40},{48,56},{64,72},{80,88},{96,104},{112,120},{... | collective-permute-start | bytes 1671176 | tf_op jit(solution)/shard_map/ppermute | solution.py:542
  4.4 20.5 %collective-permute-start.3 = (f32[64,2176]{1,0:T(8,128)S(1)}, f32[64,2176]{1,0:T(8,128)S(1)}, u32[]{:S(2)}, u32[]{:S(2)}) collective-permute-start(f32[64,2176]{1,0:T(8,128)S(1)} %get-tuple-element.35), channel_id=1, source_target_pairs={{8,16},{24,32},{40,48},{56,64},{72,80},{88,96},{104,112},{120,128}... | collective-permute-start | bytes 1671176 | tf_op jit(solution)/shard_map/ppermute | solution.py:542
  8.4 4.2 %collective-permute-start = (f32[72,128]{1,0:T(8,128)S(1)}, f32[72,128]{1,0:T(8,128)S(1)}, u32[]{:S(2)}, u32[]{:S(2)}) collective-permute-start(f32[72,128]{1,0:T(8,128)S(1)} %get-tuple-element.28), channel_id=1, source_target_pairs={{0,1},{2,3},{4,5},{6,7},{1,0},{3,2},{5,4},{7,6},{8,9},{10,11},{12,... | collective-permute-start | bytes 110600 | tf_op jit(solution)/shard_map/ppermute | solution.py:544
  9.7 5.6 %collective-permute-start.1 = (f32[72,128]{1,0:T(8,128)S(1)}, f32[72,128]{1,0:T(8,128)S(1)}, u32[]{:S(2)}, u32[]{:S(2)}) collective-permute-start(f32[72,128]{1,0:T(8,128)S(1)} %get-tuple-element.29), channel_id=1, source_target_pairs={{1,2},{3,4},{5,6},{2,1},{4,3},{6,5},{9,10},{11,12},{13,14},{10,9},... | collective-permute-start | bytes 110600 | tf_op jit(solution)/shard_map/ppermute | solution.py:544
  15.3 9.6 %collective-permute-start.4 = (f32[64,128]{1,0:T(8,128)S(1)}, f32[64,128]{1,0:T(8,128)S(1)}, u32[]{:S(2)}, u32[]{:S(2)}) collective-permute-start(f32[64,128]{1,0:T(8,128)S(1)} %get-tuple-element.36), channel_id=1, source_target_pairs={{0,8},{16,24},{32,40},{48,56},{64,72},{80,88},{96,104},{112,120},{... | collective-permute-start | bytes 98312 | tf_op jit(solution)/shard_map/ppermute | solution.py:546
  18.8 6.1 %collective-permute-start.5 = (f32[64,128]{1,0:T(8,128)S(1)}, f32[64,128]{1,0:T(8,128)S(1)}, u32[]{:S(2)}, u32[]{:S(2)}) collective-permute-start(f32[64,128]{1,0:T(8,128)S(1)} %get-tuple-element.37), channel_id=1, source_target_pairs={{8,16},{24,32},{40,48},{56,64},{72,80},{88,96},{104,112},{120,128}... | collective-permute-start | bytes 98312 | tf_op jit(solution)/shard_map/ppermute | solution.py:547
  27.2 1.3 %collective-permute-start.6 = (f32[40,128]{1,0:T(8,128)S(1)}, f32[40,128]{1,0:T(8,128)S(1)}, u32[]{:S(2)}, u32[]{:S(2)}) collective-permute-start(f32[40,128]{1,0:T(8,128)S(1)} %get-tuple-element.39), channel_id=1, source_target_pairs={{0,1},{1,0},{2,3},{3,2},{4,5},{5,4},{6,7},{7,6},{8,9},{9,8},{10,11... | collective-permute-start | bytes 61448 | tf_op jit(solution)/shard_map/ppermute | solution.py:553
  61.4 4.4 %collective-permute-start.7 = (f32[40,128]{1,0:T(8,128)S(1)}, f32[40,128]{1,0:T(8,128)S(1)}, u32[]{:S(2)}, u32[]{:S(2)}) collective-permute-start(f32[40,128]{1,0:T(8,128)S(1)} %fusion.2.refs_0_), channel_id=1, source_target_pairs={{0,1},{1,0},{2,3},{3,2},{4,5},{5,4},{6,7},{7,6},{8,9},{9,8},{10,11... | collective-permute-start | bytes 61448 | tf_op jit(solution)/shard_map/ppermute | solution.py:555

commit v3 on v2

--- a/solution.py
+++ b/solution.py
@@ -46,53 +46,9 @@
     return lax.axis_index("core") == 1
 
 
-def row_kernel(u, kap, dec, first_to, second_to, usem, ksem):
-    def send(order):
-        copies = []
-        for h, (to, near, far) in enumerate(order):
-            copies.append(pltpu.make_async_copy(u.at[:, near, :], to.at[:, 0:COLS], usem.at[h, 0]))
-            copies.append(pltpu.make_async_copy(u.at[:, far, :], to.at[:, COLS : 2 * COLS], usem.at[h, 1]))
-        for copy in copies:
-            copy.start()
-        small = []
-        for h, (to, near, _) in enumerate(order):
-            to[:, FIELD : FIELD + 128] = jnp.zeros((S, 128), F32)
-            for t in range(TILES):
-                tiles = to.at[8 * t : 8 * t + FIELDS, FIELD : FIELD + 128]
-                small.append(pltpu.make_async_copy(kap.at[:, near, tile(t)], tiles, ksem.at[h, 0, t]))
-                line = to.at[8 * t + FIELDS : 8 * t + FIELDS + 1, FIELD : FIELD + 128]
-                small.append(pltpu.make_async_copy(dec.at[near : near + 1, tile(t)], line, ksem.at[h, 1, t]))
-        for copy in small:
-            copy.start()
-        for copy in copies + small:
-            copy.wait()
-
-    odd = odd_row_device()
-    top, bottom = (0, 1), (ROWS - 1, ROWS - 2)
-
-    @pl.when(odd)
-    def _():
-        send(((first_to, *top), (second_to, *bottom)))
-
-    @pl.when(jnp.logical_not(odd))
-    def _():
-        send(((first_to, *bottom), (second_to, *top)))
-
-
-def rows(initial, kappa, decay):
-    message = pltpu.VMEM((S, MESSAGE), F32)
-    return pl.pallas_call(
-        row_kernel,
-        name="rows",
-        in_specs=[HBM] * 3,
-        out_specs=[VM] * 2,
-        out_shape=[message, message],
-        scratch_shapes=[pltpu.SemaphoreType.DMA((2, 2)), pltpu.SemaphoreType.DMA((2, 2, TILES))],
-        compiler_params=params(58),
-    )(initial, kappa, decay)
-
-
-def column_kernel(u, kap, dec, uall, west, east, first_to, second_to, sems):
+def message_kernel(u, kap, dec, index, uall, west, east, row_a, row_b, col_a, col_b, fi, sems, scalars, index_sem):
+    index_copy = pltpu.make_async_copy(index, scalars, index_sem)
+    index_copy.start()
     for x in range(ROWS):
         uall[x, S:EXT, :] = jnp.zeros((8, COLS), F32)
     copies = []
@@ -106,6 +62,13 @@
         )
         for copy in copies[x]:
             copy.start()
+    index_copy.wait()
+    sub = lax.broadcasted_iota(jnp.int32, (8, 128), 0)
+    for g in range(GROUPS):
+        v = jnp.full((8, 128), scalars[8 * g], jnp.int32)
+        for i in range(1, 8):
+            v = jnp.where(sub == i, scalars[8 * g + i], v)
+        fi[group(g), :] = v
     lane = lanes()
     w = [jnp.zeros((8, 128), F32) for _ in range(GROUPS + 1)]
     e = [jnp.zeros((8, 128), F32) for _ in range(GROUPS + 1)]
@@ -119,25 +82,36 @@
             if g < GROUPS:
                 w[g] = jnp.where(lane == ROWS + x, pltpu.roll(first, ROWS + x - 1, 1), w[g])
                 e[g] = jnp.where(lane == ROWS + x, pltpu.roll(last, ROWS + x + 2, 1), e[g])
+    odd = odd_column_device()
     for g in range(GROUPS + 1):
         west[group(g), :] = w[g]
         east[group(g), :] = e[g]
-        odd = odd_column_device()
-        first_to[group(g), :] = jnp.where(odd, w[g], e[g])
-        second_to[group(g), :] = jnp.where(odd, e[g], w[g])
-
-
-def columns(initial, kappa, decay):
-    col = pltpu.VMEM((EXT, 128), F32)
+        col_a[group(g), :] = jnp.where(odd, w[g], e[g])
+        col_b[group(g), :] = jnp.where(odd, e[g], w[g])
+    odd = odd_row_device()
+    for to, top in ((row_a, odd), (row_b, jnp.logical_not(odd))):
+        near, far = jnp.where(top, 0, ROWS - 1), jnp.where(top, 1, ROWS - 2)
+        to[:, 0:COLS] = uall[near, 0:S, :]
+        to[:, COLS : 2 * COLS] = uall[far, 0:S, :]
+        for t in range(TILES):
+            to[8 * t : 8 * t + 8, FIELD : FIELD + 128] = uall[near, S:EXT, tile(t)]
+
+
+def messages(initial, kappa, decay, field_index):
+    row, col = pltpu.VMEM((S, MESSAGE), F32), pltpu.VMEM((EXT, 128), F32)
     return pl.pallas_call(
-        column_kernel,
-        name="columns",
-        in_specs=[HBM] * 3,
-        out_specs=[VM] * 5,
-        out_shape=[pltpu.VMEM((ROWS, EXT, COLS), F32), col, col, col, col],
-        scratch_shapes=[pltpu.SemaphoreType.DMA((3, ROWS))],
-        compiler_params=params(54),
-    )(initial, kappa, decay)
+        message_kernel,
+        name="messages",
+        in_specs=[HBM] * 4,
+        out_specs=[VM] * 8,
+        out_shape=[
+            pltpu.VMEM((ROWS, EXT, COLS), F32), col, col, row, row, col, col, pltpu.VMEM((S, 128), jnp.int32),
+        ],
+        scratch_shapes=[
+            pltpu.SemaphoreType.DMA((3, ROWS)), pltpu.SMEM((S,), jnp.int32), pltpu.SemaphoreType.DMA(()),
+        ],
+        compiler_params=params(52),
+    )(initial, kappa, decay, field_index)
 
 
 def corner_kernel(first_from, second_from, halo_w, halo_e, first_to, second_to):
@@ -456,10 +430,13 @@
                 z[lo + 8 * part : lo + 8 * part + 8, tile(h)] = v
         if lo + BLOCK < SNAP:
             done = z[lo : lo + BLOCK, :]
-            update = lax.dot_general(
-                done[:, :SNAP], done, (((0,), (0,)), ((), ())),
-                precision=lax.Precision.HIGHEST, preferred_element_type=F32,
-            )
+            high = done.astype(BF16)
+            left_over = done - high.astype(F32)
+            mid = left_over.astype(BF16)
+            low = (left_over - mid.astype(F32)).astype(BF16)
+            left = jnp.concatenate([high, high, mid, high, low, mid], 0)[:, :SNAP]
+            right = jnp.concatenate([high, mid, high, low, high, mid], 0)
+            update = lax.dot_general(left, right, (((0,), (0,)), ((), ())), preferred_element_type=F32)
             m[lo + BLOCK :, :] = m[lo + BLOCK :, :] - update[lo + BLOCK :, :]
 
 
@@ -537,10 +514,8 @@
 
 
 def shards(initial, kappa, decay, field_index):
-    fi = jnp.broadcast_to(field_index[:, None], (S, 128))
-    row_a, row_b = rows(initial, kappa, decay)
+    uall, own_w, own_e, row_a, row_b, col_a, col_b, fi = messages(initial, kappa, decay, field_index)
     near_a, near_b = lax.ppermute(row_a, ROWAXIS, pairs(ROWAXIS, 0)), lax.ppermute(row_b, ROWAXIS, pairs(ROWAXIS, 1))
-    uall, own_w, own_e, col_a, col_b = columns(initial, kappa, decay)
     col_a, col_b = lax.ppermute(col_a, COLAXIS, pairs(COLAXIS, 0)), lax.ppermute(col_b, COLAXIS, pairs(COLAXIS, 1))
     halo_w, halo_e, corner_a, corner_b = corners(col_a, col_b)
     corner_a = lax.ppermute(corner_a, ROWAXIS, pairs(ROWAXIS, 0))

time: 78.8 us -> 75.7 us (0.961)
  Pallas kernels: 25.2 us -> 22.2 us
    pallas_call x2 -> x1, Pallas kernels: 4.88 us -> 3.23 us  [messages(): pl.pallas_call(message_kernel, name='messages', in_specs=[HBM] * 4, out_s...]
    pallas_call x1, Pallas kernels: 12.6 us -> 11.3 us  [make_basis(): pl.pallas_call(kernel, name='basis', in_specs=[VM] * 10, out_specs=[HBM,...]
  transfers between devices with their start and end apart: 8 -> 8, of which waited for: 3 -> 3; matrix products, arithmetic and copies ran while one was open for 0% -> 0% of each run, Pallas kernels for 11% -> 7%
where the time goes in v3:
time: 75.7 us; the launch traced here: 75.5 us
  blocking collectives  32.9 us (43%)
  Pallas kernels  22.2 us (29%)
  starting transfers between devices  14.7 us (19%)
  waiting for transfers between devices  4.74 us (6%)
  between operations  0.91 us (1%)
    all_to_all x2, blocking collectives, spread_sum(): lax.all_to_all(jnp.broadcast_to(value[None], (count, *value.shape)), axis...  32.9 us
    pallas_call x1, Pallas kernels, make_basis(): pl.pallas_call(kernel, name='basis', in_specs=[VM] * 10, out_specs=[HBM,...  11.3 us
    pallas_call x1, Pallas kernels, interior(): pl.pallas_call(interior_kernel, name='interior', in_specs=[VM] * 6, out_s...  5.37 us
    ppermute x1, starting transfers between devices, shards(): other = lax.ppermute(mine, 'core', swap)  3.54 us
    ppermute x1, starting transfers between devices, shards(): corner_a = lax.ppermute(corner_a, ROWAXIS, pairs(ROWAXIS, 0))  3.44 us
    pallas_call x1, Pallas kernels, messages(): pl.pallas_call(message_kernel, name='messages', in_specs=[HBM] * 4, out_s...  3.23 us
    ppermute x1, starting transfers between devices, shards(): lax.ppermute(col_b, COLAXIS, pairs(COLAXIS, 1))  2.83 us
    ppermute x1, waiting for transfers between devices, shards(): lax.ppermute(col_b, COLAXIS, pairs(COLAXIS, 1))  2.71 us
  transfers between devices with their start and end apart: 8, of which 3 were waited for; matrix products, arithmetic and copies ran while one was open for 0% of the time, Pallas kernels for 7%

profile of v3, /device:TPU:1, one launch (start us, length us, event | category | flops | bytes accessed | tf_op | source)
XLA Modules:
  0.0 75.5 jit_solution(17847660590002521735)
XLA Ops:
  0.6 3.2 %messages.1 = (f32[16,72,1024]{2,1,0:T(8,128)S(1)}, f32[72,128]{1,0:T(8,128)S(1)}, f32[72,128]{1,0:T(8,128)S(1)}, f32[64,2176]{1,0:T(8,128)S(1)}, f32[64,2176]{1...) custom-call(f32[64,16,1024]{2,1,0:T(8,128)} %u.1, f32[4,16,1024]{2,1,0:T(8,128)} %kap.1, ...), custom_call_target="tpu_custom_call" | custom-call | tf_op jit(solution)/shard_map/messages/pallas_call | solution.py:102
  3.9 2.1 %collective-permute-start.2 = (f32[64,2176]{1,0:T(8,128)S(1)}, f32[64,2176]{1,0:T(8,128)S(1)}, u32[]{:S(2)}, u32[]{:S(2)}) collective-permute-start(f32[64,2176]{1,0:T(8,128)S(1)} %get-tuple-element.36), channel_id=1, source_target_pairs={{0,8},{16,24},{32,40},{48,56},{64,72},{80,88},{96,104},{112,120},{... | collective-permute-start | bytes 1671176 | tf_op jit(solution)/shard_map/ppermute | solution.py:518
  6.0 0.7 collective-permute-start.3
  6.7 1.3 %collective-permute-start = (f32[72,128]{1,0:T(8,128)S(1)}, f32[72,128]{1,0:T(8,128)S(1)}, u32[]{:S(2)}, u32[]{:S(2)}) collective-permute-start(f32[72,128]{1,0:T(8,128)S(1)} %get-tuple-element.30), channel_id=1, source_target_pairs={{0,1},{2,3},{4,5},{6,7},{1,0},{3,2},{5,4},{7,6},{8,9},{10,11},{12,... | collective-permute-start | bytes 110600 | tf_op jit(solution)/shard_map/ppermute | solution.py:519
  8.0 2.8 %collective-permute-start.1 = (f32[72,128]{1,0:T(8,128)S(1)}, f32[72,128]{1,0:T(8,128)S(1)}, u32[]{:S(2)}, u32[]{:S(2)}) collective-permute-start(f32[72,128]{1,0:T(8,128)S(1)} %get-tuple-element.31), channel_id=1, source_target_pairs={{1,2},{3,4},{5,6},{2,1},{4,3},{6,5},{9,10},{11,12},{13,14},{10,9},... | collective-permute-start | bytes 110600 | tf_op jit(solution)/shard_map/ppermute | solution.py:519
  10.8 0.0 collective-permute-done.first_from
  10.8 2.7 %collective-permute-done.1.second_from = f32[72,128]{1,0:T(8,128)S(1)} collective-permute-done((f32[72,128]{1,0:T(8,128)S(1)}, f32[72,128]{1,0:T(8,128)S(1)}, u32[]{:S(2)}, u32[]{:S(2)}) %collective-permute-start.1) | collective-permute-done | bytes 36896 | tf_op jit(solution)/shard_map/ppermute | solution.py:519
  13.6 0.1 corners.1
  13.7 3.4 %collective-permute-start.4 = (f32[64,128]{1,0:T(8,128)S(1)}, f32[64,128]{1,0:T(8,128)S(1)}, u32[]{:S(2)}, u32[]{:S(2)}) collective-permute-start(f32[64,128]{1,0:T(8,128)S(1)} %get-tuple-element.38), channel_id=1, source_target_pairs={{0,8},{16,24},{32,40},{48,56},{64,72},{80,88},{96,104},{112,120},{... | collective-permute-start | bytes 98312 | tf_op jit(solution)/shard_map/ppermute | solution.py:521
  17.1 0.7 collective-permute-start.5
  17.8 5.4 %interior.1 = (f32[16,64,1024]{2,1,0:T(8,128)S(1)}, bf16[4,128,1024]{2,1,0:T(8,128)(2,1)S(1)}, bf16[4,128,1024]{2,1,0:T(8,128)(2,1)S(1)}, bf16[4,128,1024]{2,1,0...) custom-call(s32[64,128]{1,0:T(8,128)S(1)} %get-tuple-element.26.fi, ...), custom_call_target="tpu_custom_call" | custom-call | flops 805306368 | bytes 33554432 | tf_op jit(solution)/shard_map/interior/pallas_call | solution.py:275
  23.1 0.0 collective-permute-done.4.nc
  23.1 0.0 collective-permute-done.5.sc
  23.2 0.0 collective-permute-done.2.n1
  23.2 0.0 collective-permute-done.3.s1
  23.2 2.3 %edges.1 = (bf16[4,128,1024]{2,1,0:T(8,128)(2,1)S(1)}, bf16[4,128,1024]{2,1,0:T(8,128)(2,1)S(1)}, f32[40,128]{1,0:T(8,128)S(1)}, f32[40,128]{1,0:T(8,128)S(1)}) custom-call(s32[64,128]{1,0:T(8,128)S(1)} %get-tuple-element.26.fi, f32[16,72,1024]{2,1,0:T(8,128)S(1)} %get-tuple-element.27.uall, f32[72,128]{1,0:T(8,128)S(1)} %get-tuple-element.28.own_w, ...), custom_call_target="tpu_custom_call" | custom-call | tf_op jit(solution)/shard_map/edges/pallas_call | solution.py:378
  25.4 0.1 collective-permute-start.6
  25.5 1.2 %collective-permute-done.6 = f32[40,128]{1,0:T(8,128)S(1)} collective-permute-done((f32[40,128]{1,0:T(8,128)S(1)}, f32[40,128]{1,0:T(8,128)S(1)}, u32[]{:S(2)}, u32[]{:S(2)}) %collective-permute-start.6) | collective-permute-done | bytes 20512 | tf_op jit(solution)/shard_map/ppermute | solution.py:528
  26.8 17.1 %all_to_all.10 = f32[16,40,128]{2,1,0:T(8,128)S(1)} all-to-all(f32[16,40,128]{2,1,0:T(8,128)S(1)} %broadcast_in_dim.6), channel_id=1, replica_groups=mesh['z'=8,'x'=4,'y'=4,'core'=2] {'x','y'}, dimensions={0} | all-to-all | bytes 655360 | tf_op jit(solution)/shard_map/all_to_all | solution.py:504
  43.9 15.8 %all_to_all.11 = f32[8,40,128]{2,1,0:T(8,128)S(1)} all-to-all(f32[8,40,128]{2,1,0:T(8,128)S(1)} %broadcast_in_dim.16), channel_id=1, replica_groups=mesh['z'=8,'x'=4,'y'=4,'core'=2] {'z'}, dimensions={0} | all-to-all | bytes 327680 | tf_op jit(solution)/shard_map/all_to_all | solution.py:504
  59.7 3.5 %collective-permute-start.7 = (f32[40,128]{1,0:T(8,128)S(1)}, f32[40,128]{1,0:T(8,128)S(1)}, u32[]{:S(2)}, u32[]{:S(2)}) collective-permute-start(f32[40,128]{1,0:T(8,128)S(1)} %fusion.2.refs_0_), channel_id=1, source_target_pairs={{0,1},{1,0},{2,3},{3,2},{4,5},{5,4},{6,7},{7,6},{8,9},{9,8},{10,11... | collective-permute-start | bytes 61448 | tf_op jit(solution)/shard_map/ppermute | solution.py:530
  63.2 0.8 %collective-permute-done.7.refs_1_ = f32[40,128]{1,0:T(8,128)S(1)} collective-permute-done((f32[40,128]{1,0:T(8,128)S(1)}, f32[40,128]{1,0:T(8,128)S(1)}, u32[]{:S(2)}, u32[]{:S(2)}) %collective-permute-start.7) | collective-permute-done | bytes 20512 | tf_op jit(solution)/shard_map/ppermute | solution.py:530
  64.1 11.3 %basis.1 = (f32[128,16,1024]{2,1,0:T(8,128)}, f32[128,128]{1,0:T(8,128)}) custom-call(f32[40,128]{1,0:T(8,128)S(1)} %fusion.2.refs_0_, f32[40,128]{1,0:T(8,128)S(1)} %collective-permute-done.7.refs_1_, bf16[4,128,1024]{2,1,0:T(8,128)(2,1)S(1)} %get-tuple-element.42.refs_2_, bf16[4,128,1024]{2,1,0:T(8,128)(2,1)S(1)} %get-tuple-element.43.refs_3_, ...), custom_call_target="tpu_custom_call" | custom-call | tf_op jit(solution)/shard_map/basis/pallas_call | solution.py:483
  (5 shorter events, 0.1 us)
Async XLA Ops:
  3.9 19.3 %collective-permute-start.2 = (f32[64,2176]{1,0:T(8,128)S(1)}, f32[64,2176]{1,0:T(8,128)S(1)}, u32[]{:S(2)}, u32[]{:S(2)}) collective-permute-start(f32[64,2176]{1,0:T(8,128)S(1)} %get-tuple-element.36), channel_id=1, source_target_pairs={{0,8},{16,24},{32,40},{48,56},{64,72},{80,88},{96,104},{112,120},{... | collective-permute-start | bytes 1671176 | tf_op jit(solution)/shard_map/ppermute | solution.py:518
  6.0 17.2 %collective-permute-start.3 = (f32[64,2176]{1,0:T(8,128)S(1)}, f32[64,2176]{1,0:T(8,128)S(1)}, u32[]{:S(2)}, u32[]{:S(2)}) collective-permute-start(f32[64,2176]{1,0:T(8,128)S(1)} %get-tuple-element.37), channel_id=1, source_target_pairs={{8,16},{24,32},{40,48},{56,64},{72,80},{88,96},{104,112},{120,128}... | collective-permute-start | bytes 1671176 | tf_op jit(solution)/shard_map/ppermute | solution.py:518
  6.7 4.2 %collective-permute-start = (f32[72,128]{1,0:T(8,128)S(1)}, f32[72,128]{1,0:T(8,128)S(1)}, u32[]{:S(2)}, u32[]{:S(2)}) collective-permute-start(f32[72,128]{1,0:T(8,128)S(1)} %get-tuple-element.30), channel_id=1, source_target_pairs={{0,1},{2,3},{4,5},{6,7},{1,0},{3,2},{5,4},{7,6},{8,9},{10,11},{12,... | collective-permute-start | bytes 110600 | tf_op jit(solution)/shard_map/ppermute | solution.py:519
  8.0 5.6 %collective-permute-start.1 = (f32[72,128]{1,0:T(8,128)S(1)}, f32[72,128]{1,0:T(8,128)S(1)}, u32[]{:S(2)}, u32[]{:S(2)}) collective-permute-start(f32[72,128]{1,0:T(8,128)S(1)} %get-tuple-element.31), channel_id=1, source_target_pairs={{1,2},{3,4},{5,6},{2,1},{4,3},{6,5},{9,10},{11,12},{13,14},{10,9},... | collective-permute-start | bytes 110600 | tf_op jit(solution)/shard_map/ppermute | solution.py:519
  13.7 9.5 %collective-permute-start.4 = (f32[64,128]{1,0:T(8,128)S(1)}, f32[64,128]{1,0:T(8,128)S(1)}, u32[]{:S(2)}, u32[]{:S(2)}) collective-permute-start(f32[64,128]{1,0:T(8,128)S(1)} %get-tuple-element.38), channel_id=1, source_target_pairs={{0,8},{16,24},{32,40},{48,56},{64,72},{80,88},{96,104},{112,120},{... | collective-permute-start | bytes 98312 | tf_op jit(solution)/shard_map/ppermute | solution.py:521
  17.1 6.0 %collective-permute-start.5 = (f32[64,128]{1,0:T(8,128)S(1)}, f32[64,128]{1,0:T(8,128)S(1)}, u32[]{:S(2)}, u32[]{:S(2)}) collective-permute-start(f32[64,128]{1,0:T(8,128)S(1)} %get-tuple-element.39), channel_id=1, source_target_pairs={{8,16},{24,32},{40,48},{56,64},{72,80},{88,96},{104,112},{120,128}... | collective-permute-start | bytes 98312 | tf_op jit(solution)/shard_map/ppermute | solution.py:522
  25.4 1.3 %collective-permute-start.6 = (f32[40,128]{1,0:T(8,128)S(1)}, f32[40,128]{1,0:T(8,128)S(1)}, u32[]{:S(2)}, u32[]{:S(2)}) collective-permute-start(f32[40,128]{1,0:T(8,128)S(1)} %get-tuple-element.41), channel_id=1, source_target_pairs={{0,1},{1,0},{2,3},{3,2},{4,5},{5,4},{6,7},{7,6},{8,9},{9,8},{10,11... | collective-permute-start | bytes 61448 | tf_op jit(solution)/shard_map/ppermute | solution.py:528
  59.7 4.4 %collective-permute-start.7 = (f32[40,128]{1,0:T(8,128)S(1)}, f32[40,128]{1,0:T(8,128)S(1)}, u32[]{:S(2)}, u32[]{:S(2)}) collective-permute-start(f32[40,128]{1,0:T(8,128)S(1)} %fusion.2.refs_0_), channel_id=1, source_target_pairs={{0,1},{1,0},{2,3},{3,2},{4,5},{5,4},{6,7},{7,6},{8,9},{9,8},{10,11... | collective-permute-start | bytes 61448 | tf_op jit(solution)/shard_map/ppermute | solution.py:530

commit v4 on v3

--- a/solution.py
+++ b/solution.py
@@ -508,6 +508,13 @@
     return parts[0]
 
 
+def swap_sum(value, axis, *offsets):
+    count = lax.axis_size(axis)
+    got = [lax.ppermute(value, axis, [(i, i ^ k) for i in range(count)]) for k in offsets]
+    total = value + got[0]
+    return total if len(got) == 1 else total + (got[1] + got[2])
+
+
 def pairs(axis, start):
     lower = range(start, lax.axis_size(axis) - 1, 2)
     return [(i, i + 1) for i in lower] + [(i + 1, i) for i in lower]
@@ -526,7 +533,8 @@
     )
     swap = [(0, 1), (1, 0)]
     mine = keep + lax.ppermute(give, "core", swap)
-    mine = spread_sum(spread_sum(mine, ("x", "y")), "z")
+    mine = swap_sum(swap_sum(mine, "x", 1, 3, 2), "y", 1, 3, 2)
+    mine = swap_sum(swap_sum(mine, "z", 1, 3, 2), "z", 7)
     other = lax.ppermute(mine, "core", swap)
     cells = lax.axis_size(ROWAXIS) * lax.axis_size(COLAXIS) * ROWS * COLS
     return make_basis(math.sqrt(cells), mine, other, *inner_snaps, edge_f, edge_s)

time: 75.7 us -> 73.6 us (0.972)
  blocking collectives: 32.9 us -> 0 us
  starting transfers between devices: 14.7 us -> 35.3 us
  waiting for transfers between devices: 4.74 us -> 14.9 us
    all_to_all x2 -> x0, blocking collectives: 32.9 us -> none  [spread_sum(): lax.all_to_all(jnp.broadcast_to(value[None], (count, *value.shape)), axis...]
    ppermute x0 -> x10, starting transfers between devices: none -> 18.5 us  [swap_sum(): lax.ppermute(value, axis, [(i, i ^ k) for i in range(count)])]
    ppermute x0 -> x10, waiting for transfers between devices: none -> 10.2 us  [swap_sum(): lax.ppermute(value, axis, [(i, i ^ k) for i in range(count)])]
    ppermute x1, starting transfers between devices: 3.54 us -> 5.71 us  [shards(): other = lax.ppermute(mine, 'core', swap)]
  transfers between devices with their start and end apart: 8 -> 18, of which waited for: 3 -> 10; matrix products, arithmetic and copies ran while one was open for 0% -> 0% of each run, Pallas kernels for 7% -> 7%
where the time goes in v4:
time: 73.6 us; the launch traced here: 73.4 us
  starting transfers between devices  35.3 us (48%)
  Pallas kernels  22.2 us (30%)
  waiting for transfers between devices  14.9 us (20%)
  between operations  0.91 us (1%)
    ppermute x10, starting transfers between devices, swap_sum(): lax.ppermute(value, axis, [(i, i ^ k) for i in range(count)])  18.5 us
    pallas_call x1, Pallas kernels, make_basis(): pl.pallas_call(kernel, name='basis', in_specs=[VM] * 10, out_specs=[HBM,...  11.3 us
    ppermute x10, waiting for transfers between devices, swap_sum(): lax.ppermute(value, axis, [(i, i ^ k) for i in range(count)])  10.2 us
    ppermute x1, starting transfers between devices, shards(): other = lax.ppermute(mine, 'core', swap)  5.71 us
    pallas_call x1, Pallas kernels, interior(): pl.pallas_call(interior_kernel, name='interior', in_specs=[VM] * 6, out_s...  5.37 us
    ppermute x1, starting transfers between devices, shards(): corner_a = lax.ppermute(corner_a, ROWAXIS, pairs(ROWAXIS, 0))  3.44 us
    pallas_call x1, Pallas kernels, messages(): pl.pallas_call(message_kernel, name='messages', in_specs=[HBM] * 4, out_s...  3.23 us
    ppermute x1, starting transfers between devices, shards(): lax.ppermute(col_b, COLAXIS, pairs(COLAXIS, 1))  2.83 us
  transfers between devices with their start and end apart: 18, of which 10 were waited for; matrix products, arithmetic and copies ran while one was open for 0% of the time, Pallas kernels for 7%

profile of v4, /device:TPU:1, one launch (start us, length us, event | category | flops | bytes accessed | tf_op | source)
XLA Modules:
  0.0 73.4 jit_solution(1188107665401043692)
XLA Ops:
  0.6 3.2 %messages.1 = (f32[16,72,1024]{2,1,0:T(8,128)S(1)}, f32[72,128]{1,0:T(8,128)S(1)}, f32[72,128]{1,0:T(8,128)S(1)}, f32[64,2176]{1,0:T(8,128)S(1)}, f32[64,2176]{1...) custom-call(f32[64,16,1024]{2,1,0:T(8,128)} %u.1, f32[4,16,1024]{2,1,0:T(8,128)} %kap.1, ...), custom_call_target="tpu_custom_call" | custom-call | tf_op jit(solution)/shard_map/messages/pallas_call | solution.py:102
  3.9 2.1 %collective-permute-start.2 = (f32[64,2176]{1,0:T(8,128)S(1)}, f32[64,2176]{1,0:T(8,128)S(1)}, u32[]{:S(2)}, u32[]{:S(2)}) collective-permute-start(f32[64,2176]{1,0:T(8,128)S(1)} %get-tuple-element.36), channel_id=1, source_target_pairs={{0,8},{16,24},{32,40},{48,56},{64,72},{80,88},{96,104},{112,120},{... | collective-permute-start | bytes 1671176 | tf_op jit(solution)/shard_map/ppermute | solution.py:525
  6.0 0.7 collective-permute-start.3
  6.7 1.3 %collective-permute-start = (f32[72,128]{1,0:T(8,128)S(1)}, f32[72,128]{1,0:T(8,128)S(1)}, u32[]{:S(2)}, u32[]{:S(2)}) collective-permute-start(f32[72,128]{1,0:T(8,128)S(1)} %get-tuple-element.30), channel_id=1, source_target_pairs={{0,1},{2,3},{4,5},{6,7},{1,0},{3,2},{5,4},{7,6},{8,9},{10,11},{12,... | collective-permute-start | bytes 110600 | tf_op jit(solution)/shard_map/ppermute | solution.py:526
  8.0 2.8 %collective-permute-start.1 = (f32[72,128]{1,0:T(8,128)S(1)}, f32[72,128]{1,0:T(8,128)S(1)}, u32[]{:S(2)}, u32[]{:S(2)}) collective-permute-start(f32[72,128]{1,0:T(8,128)S(1)} %get-tuple-element.31), channel_id=1, source_target_pairs={{1,2},{3,4},{5,6},{2,1},{4,3},{6,5},{9,10},{11,12},{13,14},{10,9},... | collective-permute-start | bytes 110600 | tf_op jit(solution)/shard_map/ppermute | solution.py:526
  10.8 0.0 collective-permute-done.first_from
  10.8 2.7 %collective-permute-done.1.second_from = f32[72,128]{1,0:T(8,128)S(1)} collective-permute-done((f32[72,128]{1,0:T(8,128)S(1)}, f32[72,128]{1,0:T(8,128)S(1)}, u32[]{:S(2)}, u32[]{:S(2)}) %collective-permute-start.1) | collective-permute-done | bytes 36896 | tf_op jit(solution)/shard_map/ppermute | solution.py:526
  13.6 0.1 corners.1
  13.7 3.4 %collective-permute-start.4 = (f32[64,128]{1,0:T(8,128)S(1)}, f32[64,128]{1,0:T(8,128)S(1)}, u32[]{:S(2)}, u32[]{:S(2)}) collective-permute-start(f32[64,128]{1,0:T(8,128)S(1)} %get-tuple-element.38), channel_id=1, source_target_pairs={{0,8},{16,24},{32,40},{48,56},{64,72},{80,88},{96,104},{112,120},{... | collective-permute-start | bytes 98312 | tf_op jit(solution)/shard_map/ppermute | solution.py:528
  17.1 0.7 collective-permute-start.5
  17.8 5.4 %interior.1 = (f32[16,64,1024]{2,1,0:T(8,128)S(1)}, bf16[4,128,1024]{2,1,0:T(8,128)(2,1)S(1)}, bf16[4,128,1024]{2,1,0:T(8,128)(2,1)S(1)}, bf16[4,128,1024]{2,1,0...) custom-call(s32[64,128]{1,0:T(8,128)S(1)} %get-tuple-element.26.fi, ...), custom_call_target="tpu_custom_call" | custom-call | flops 805306368 | bytes 33554432 | tf_op jit(solution)/shard_map/interior/pallas_call | solution.py:275
  23.1 0.0 collective-permute-done.4.nc
  23.1 0.0 collective-permute-done.5.sc
  23.2 0.0 collective-permute-done.2.n1
  23.2 0.0 collective-permute-done.3.s1
  23.2 2.3 %edges.1 = (bf16[4,128,1024]{2,1,0:T(8,128)(2,1)S(1)}, bf16[4,128,1024]{2,1,0:T(8,128)(2,1)S(1)}, f32[40,128]{1,0:T(8,128)S(1)}, f32[40,128]{1,0:T(8,128)S(1)}) custom-call(s32[64,128]{1,0:T(8,128)S(1)} %get-tuple-element.26.fi, f32[16,72,1024]{2,1,0:T(8,128)S(1)} %get-tuple-element.27.uall, f32[72,128]{1,0:T(8,128)S(1)} %get-tuple-element.28.own_w, ...), custom_call_target="tpu_custom_call" | custom-call | tf_op jit(solution)/shard_map/edges/pallas_call | solution.py:378
  25.4 0.1 collective-permute-start.6
  25.5 1.2 %collective-permute-done.6 = f32[40,128]{1,0:T(8,128)S(1)} collective-permute-done((f32[40,128]{1,0:T(8,128)S(1)}, f32[40,128]{1,0:T(8,128)S(1)}, u32[]{:S(2)}, u32[]{:S(2)}) %collective-permute-start.6) | collective-permute-done | bytes 20512 | tf_op jit(solution)/shard_map/ppermute | solution.py:535
  26.7 4.3 %collective-permute-start.9 = (f32[40,128]{1,0:T(8,128)S(1)}, f32[40,128]{1,0:T(8,128)S(1)}, u32[]{:S(2)}, u32[]{:S(2)}) collective-permute-start(f32[40,128]{1,0:T(8,128)S(1)} %add.33), channel_id=1, source_target_pairs={{0,16},{8,24},{16,0},{24,8},{1,17},{9,25},{17,1},{25,9},{2,18},{10... | collective-permute-start | bytes 61448 | tf_op jit(solution)/shard_map/ppermute | solution.py:513
  31.1 2.1 %collective-permute-start.8 = (f32[40,128]{1,0:T(8,128)S(1)}, f32[40,128]{1,0:T(8,128)S(1)}, u32[]{:S(2)}, u32[]{:S(2)}) collective-permute-start(f32[40,128]{1,0:T(8,128)S(1)} %add.33), channel_id=1, source_target_pairs={{0,24},{8,16},{16,8},{24,0},{1,25},{9,17},{17,9},{25,1},{2,26},{10... | collective-permute-start | bytes 61448 | tf_op jit(solution)/shard_map/ppermute | solution.py:513
  33.1 0.0 collective-permute-start.7
  33.1 0.0 collective-permute-done.9
  33.1 1.8 %collective-permute-done.8 = f32[40,128]{1,0:T(8,128)S(1)} collective-permute-done((f32[40,128]{1,0:T(8,128)S(1)}, f32[40,128]{1,0:T(8,128)S(1)}, u32[]{:S(2)}, u32[]{:S(2)}) %collective-permute-start.8) | collective-permute-done | bytes 20512 | tf_op jit(solution)/shard_map/ppermute | solution.py:513
  34.9 1.1 %collective-permute-done.7 = f32[40,128]{1,0:T(8,128)S(1)} collective-permute-done((f32[40,128]{1,0:T(8,128)S(1)}, f32[40,128]{1,0:T(8,128)S(1)}, u32[]{:S(2)}, u32[]{:S(2)}) %collective-permute-start.7) | collective-permute-done | bytes 20512 | tf_op jit(solution)/shard_map/ppermute | solution.py:513
  36.1 3.0 %collective-permute-start.12 = (f32[40,128]{1,0:T(8,128)S(1)}, f32[40,128]{1,0:T(8,128)S(1)}, u32[]{:S(2)}, u32[]{:S(2)}) collective-permute-start(f32[40,128]{1,0:T(8,128)S(1)} %add_add_fusion.2), channel_id=1, source_target_pairs={{0,4},{2,6},{4,0},{6,2},{1,5},{3,7},{5,1},{7,3},{8,12},{10,14},{12... | collective-permute-start | bytes 61448 | tf_op jit(solution)/shard_map/ppermute | solution.py:513
  39.1 0.8 %collective-permute-start.11 = (f32[40,128]{1,0:T(8,128)S(1)}, f32[40,128]{1,0:T(8,128)S(1)}, u32[]{:S(2)}, u32[]{:S(2)}) collective-permute-start(f32[40,128]{1,0:T(8,128)S(1)} %add_add_fusion.2), channel_id=1, source_target_pairs={{0,6},{2,4},{4,2},{6,0},{1,7},{3,5},{5,3},{7,1},{8,14},{10,12},{12... | collective-permute-start | bytes 61448 | tf_op jit(solution)/shard_map/ppermute | solution.py:513
  39.8 0.0 collective-permute-start.10
  39.8 0.4 collective-permute-done.12
  40.3 2.6 %collective-permute-done.11 = f32[40,128]{1,0:T(8,128)S(1)} collective-permute-done((f32[40,128]{1,0:T(8,128)S(1)}, f32[40,128]{1,0:T(8,128)S(1)}, u32[]{:S(2)}, u32[]{:S(2)}) %collective-permute-start.11) | collective-permute-done | bytes 20512 | tf_op jit(solution)/shard_map/ppermute | solution.py:513
  42.9 0.0 collective-permute-done.10
  42.9 3.3 %collective-permute-start.15 = (f32[40,128]{1,0:T(8,128)S(1)}, f32[40,128]{1,0:T(8,128)S(1)}, u32[]{:S(2)}, u32[]{:S(2)}) collective-permute-start(f32[40,128]{1,0:T(8,128)S(1)} %add_add_fusion.1), channel_id=1, source_target_pairs={{0,64},{32,96},{64,0},{96,32},{128,192},{160,224},{192,128},{224,1... | collective-permute-start | bytes 61448 | tf_op jit(solution)/shard_map/ppermute | solution.py:513
  46.2 2.7 %collective-permute-start.14 = (f32[40,128]{1,0:T(8,128)S(1)}, f32[40,128]{1,0:T(8,128)S(1)}, u32[]{:S(2)}, u32[]{:S(2)}) collective-permute-start(f32[40,128]{1,0:T(8,128)S(1)} %add_add_fusion.1), channel_id=1, source_target_pairs={{0,96},{32,64},{64,32},{96,0},{128,224},{160,192},{192,160},{224,1... | collective-permute-start | bytes 61448 | tf_op jit(solution)/shard_map/ppermute | solution.py:513
  48.8 0.2 collective-permute-start.13
  49.0 0.0 collective-permute-done.15
  49.0 1.6 %collective-permute-done.14 = f32[40,128]{1,0:T(8,128)S(1)} collective-permute-done((f32[40,128]{1,0:T(8,128)S(1)}, f32[40,128]{1,0:T(8,128)S(1)}, u32[]{:S(2)}, u32[]{:S(2)}) %collective-permute-start.14) | collective-permute-done | bytes 20512 | tf_op jit(solution)/shard_map/ppermute | solution.py:513
  50.6 0.8 %collective-permute-done.13 = f32[40,128]{1,0:T(8,128)S(1)} collective-permute-done((f32[40,128]{1,0:T(8,128)S(1)}, f32[40,128]{1,0:T(8,128)S(1)}, u32[]{:S(2)}, u32[]{:S(2)}) %collective-permute-start.13) | collective-permute-done | bytes 20512 | tf_op jit(solution)/shard_map/ppermute | solution.py:513
  51.5 2.2 %collective-permute-start.16 = (f32[40,128]{1,0:T(8,128)S(1)}, f32[40,128]{1,0:T(8,128)S(1)}, u32[]{:S(2)}, u32[]{:S(2)}) collective-permute-start(f32[40,128]{1,0:T(8,128)S(1)} %add_add_fusion), channel_id=1, source_target_pairs={{0,224},{32,192},{64,160},{96,128},{128,96},{160,64},{192,32},{224... | collective-permute-start | bytes 61448 | tf_op jit(solution)/shard_map/ppermute | solution.py:513
  53.7 1.7 %collective-permute-done.16 = f32[40,128]{1,0:T(8,128)S(1)} collective-permute-done((f32[40,128]{1,0:T(8,128)S(1)}, f32[40,128]{1,0:T(8,128)S(1)}, u32[]{:S(2)}, u32[]{:S(2)}) %collective-permute-start.16) | collective-permute-done | bytes 20512 | tf_op jit(solution)/shard_map/ppermute | solution.py:513
  55.4 5.7 %collective-permute-start.17 = (f32[40,128]{1,0:T(8,128)S(1)}, f32[40,128]{1,0:T(8,128)S(1)}, u32[]{:S(2)}, u32[]{:S(2)}) collective-permute-start(f32[40,128]{1,0:T(8,128)S(1)} %add.43.refs_0_), channel_id=1, source_target_pairs={{0,1},{1,0},{2,3},{3,2},{4,5},{5,4},{6,7},{7,6},{8,9},{9,8},{10,11... | collective-permute-start | bytes 61448 | tf_op jit(solution)/shard_map/ppermute | solution.py:538
  61.1 0.8 %collective-permute-done.17.refs_1_ = f32[40,128]{1,0:T(8,128)S(1)} collective-permute-done((f32[40,128]{1,0:T(8,128)S(1)}, f32[40,128]{1,0:T(8,128)S(1)}, u32[]{:S(2)}, u32[]{:S(2)}) %collective-permute-start.17) | collective-permute-done | bytes 20512 | tf_op jit(solution)/shard_map/ppermute | solution.py:538
  62.0 11.3 %basis.1 = (f32[128,16,1024]{2,1,0:T(8,128)}, f32[128,128]{1,0:T(8,128)}) custom-call(f32[40,128]{1,0:T(8,128)S(1)} %add.43.refs_0_, f32[40,128]{1,0:T(8,128)S(1)} %collective-permute-done.17.refs_1_, bf16[4,128,1024]{2,1,0:T(8,128)(2,1)S(1)} %get-tuple-element.42.refs_2_, bf16[4,128,1024]{2,1,0:T(8,128)(2,1)S(1)} %get-tuple-element.43.refs_3_, ...), custom_call_target="tpu_custom_call" | custom-call | tf_op jit(solution)/shard_map/basis/pallas_call | solution.py:483
  (5 shorter events, 0.0 us)
Async XLA Ops:
  3.9 19.3 %collective-permute-start.2 = (f32[64,2176]{1,0:T(8,128)S(1)}, f32[64,2176]{1,0:T(8,128)S(1)}, u32[]{:S(2)}, u32[]{:S(2)}) collective-permute-start(f32[64,2176]{1,0:T(8,128)S(1)} %get-tuple-element.36), channel_id=1, source_target_pairs={{0,8},{16,24},{32,40},{48,56},{64,72},{80,88},{96,104},{112,120},{... | collective-permute-start | bytes 1671176 | tf_op jit(solution)/shard_map/ppermute | solution.py:525
  6.0 17.2 %collective-permute-start.3 = (f32[64,2176]{1,0:T(8,128)S(1)}, f32[64,2176]{1,0:T(8,128)S(1)}, u32[]{:S(2)}, u32[]{:S(2)}) collective-permute-start(f32[64,2176]{1,0:T(8,128)S(1)} %get-tuple-element.37), channel_id=1, source_target_pairs={{8,16},{24,32},{40,48},{56,64},{72,80},{88,96},{104,112},{120,128}... | collective-permute-start | bytes 1671176 | tf_op jit(solution)/shard_map/ppermute | solution.py:525
  6.7 4.2 %collective-permute-start = (f32[72,128]{1,0:T(8,128)S(1)}, f32[72,128]{1,0:T(8,128)S(1)}, u32[]{:S(2)}, u32[]{:S(2)}) collective-permute-start(f32[72,128]{1,0:T(8,128)S(1)} %get-tuple-element.30), channel_id=1, source_target_pairs={{0,1},{2,3},{4,5},{6,7},{1,0},{3,2},{5,4},{7,6},{8,9},{10,11},{12,... | collective-permute-start | bytes 110600 | tf_op jit(solution)/shard_map/ppermute | solution.py:526
  8.0 5.6 %collective-permute-start.1 = (f32[72,128]{1,0:T(8,128)S(1)}, f32[72,128]{1,0:T(8,128)S(1)}, u32[]{:S(2)}, u32[]{:S(2)}) collective-permute-start(f32[72,128]{1,0:T(8,128)S(1)} %get-tuple-element.31), channel_id=1, source_target_pairs={{1,2},{3,4},{5,6},{2,1},{4,3},{6,5},{9,10},{11,12},{13,14},{10,9},... | collective-permute-start | bytes 110600 | tf_op jit(solution)/shard_map/ppermute | solution.py:526
  13.7 9.5 %collective-permute-start.4 = (f32[64,128]{1,0:T(8,128)S(1)}, f32[64,128]{1,0:T(8,128)S(1)}, u32[]{:S(2)}, u32[]{:S(2)}) collective-permute-start(f32[64,128]{1,0:T(8,128)S(1)} %get-tuple-element.38), channel_id=1, source_target_pairs={{0,8},{16,24},{32,40},{48,56},{64,72},{80,88},{96,104},{112,120},{... | collective-permute-start | bytes 98312 | tf_op jit(solution)/shard_map/ppermute | solution.py:528
  17.1 6.0 %collective-permute-start.5 = (f32[64,128]{1,0:T(8,128)S(1)}, f32[64,128]{1,0:T(8,128)S(1)}, u32[]{:S(2)}, u32[]{:S(2)}) collective-permute-start(f32[64,128]{1,0:T(8,128)S(1)} %get-tuple-element.39), channel_id=1, source_target_pairs={{8,16},{24,32},{40,48},{56,64},{72,80},{88,96},{104,112},{120,128}... | collective-permute-start | bytes 98312 | tf_op jit(solution)/shard_map/ppermute | solution.py:529
  25.4 1.3 %collective-permute-start.6 = (f32[40,128]{1,0:T(8,128)S(1)}, f32[40,128]{1,0:T(8,128)S(1)}, u32[]{:S(2)}, u32[]{:S(2)}) collective-permute-start(f32[40,128]{1,0:T(8,128)S(1)} %get-tuple-element.41), channel_id=1, source_target_pairs={{0,1},{1,0},{2,3},{3,2},{4,5},{5,4},{6,7},{7,6},{8,9},{9,8},{10,11... | collective-permute-start | bytes 61448 | tf_op jit(solution)/shard_map/ppermute | solution.py:535
  26.7 6.4 %collective-permute-start.9 = (f32[40,128]{1,0:T(8,128)S(1)}, f32[40,128]{1,0:T(8,128)S(1)}, u32[]{:S(2)}, u32[]{:S(2)}) collective-permute-start(f32[40,128]{1,0:T(8,128)S(1)} %add.33), channel_id=1, source_target_pairs={{0,16},{8,24},{16,0},{24,8},{1,17},{9,25},{17,1},{25,9},{2,18},{10... | collective-permute-start | bytes 61448 | tf_op jit(solution)/shard_map/ppermute | solution.py:513
  31.1 3.8 %collective-permute-start.8 = (f32[40,128]{1,0:T(8,128)S(1)}, f32[40,128]{1,0:T(8,128)S(1)}, u32[]{:S(2)}, u32[]{:S(2)}) collective-permute-start(f32[40,128]{1,0:T(8,128)S(1)} %add.33), channel_id=1, source_target_pairs={{0,24},{8,16},{16,8},{24,0},{1,25},{9,17},{17,9},{25,1},{2,26},{10... | collective-permute-start | bytes 61448 | tf_op jit(solution)/shard_map/ppermute | solution.py:513
  33.1 2.9 %collective-permute-start.7 = (f32[40,128]{1,0:T(8,128)S(1)}, f32[40,128]{1,0:T(8,128)S(1)}, u32[]{:S(2)}, u32[]{:S(2)}) collective-permute-start(f32[40,128]{1,0:T(8,128)S(1)} %add.33), channel_id=1, source_target_pairs={{0,8},{8,0},{16,24},{24,16},{1,9},{9,1},{17,25},{25,17},{2,10},{10... | collective-permute-start | bytes 61448 | tf_op jit(solution)/shard_map/ppermute | solution.py:513
  36.1 4.2 %collective-permute-start.12 = (f32[40,128]{1,0:T(8,128)S(1)}, f32[40,128]{1,0:T(8,128)S(1)}, u32[]{:S(2)}, u32[]{:S(2)}) collective-permute-start(f32[40,128]{1,0:T(8,128)S(1)} %add_add_fusion.2), channel_id=1, source_target_pairs={{0,4},{2,6},{4,0},{6,2},{1,5},{3,7},{5,1},{7,3},{8,12},{10,14},{12... | collective-permute-start | bytes 61448 | tf_op jit(solution)/shard_map/ppermute | solution.py:513
  39.1 3.8 %collective-permute-start.11 = (f32[40,128]{1,0:T(8,128)S(1)}, f32[40,128]{1,0:T(8,128)S(1)}, u32[]{:S(2)}, u32[]{:S(2)}) collective-permute-start(f32[40,128]{1,0:T(8,128)S(1)} %add_add_fusion.2), channel_id=1, source_target_pairs={{0,6},{2,4},{4,2},{6,0},{1,7},{3,5},{5,3},{7,1},{8,14},{10,12},{12... | collective-permute-start | bytes 61448 | tf_op jit(solution)/shard_map/ppermute | solution.py:513
  39.8 3.1 %collective-permute-start.10 = (f32[40,128]{1,0:T(8,128)S(1)}, f32[40,128]{1,0:T(8,128)S(1)}, u32[]{:S(2)}, u32[]{:S(2)}) collective-permute-start(f32[40,128]{1,0:T(8,128)S(1)} %add_add_fusion.2), channel_id=1, source_target_pairs={{0,2},{2,0},{4,6},{6,4},{1,3},{3,1},{5,7},{7,5},{8,10},{10,8},{12,... | collective-permute-start | bytes 61448 | tf_op jit(solution)/shard_map/ppermute | solution.py:513
  42.9 6.1 %collective-permute-start.15 = (f32[40,128]{1,0:T(8,128)S(1)}, f32[40,128]{1,0:T(8,128)S(1)}, u32[]{:S(2)}, u32[]{:S(2)}) collective-permute-start(f32[40,128]{1,0:T(8,128)S(1)} %add_add_fusion.1), channel_id=1, source_target_pairs={{0,64},{32,96},{64,0},{96,32},{128,192},{160,224},{192,128},{224,1... | collective-permute-start | bytes 61448 | tf_op jit(solution)/shard_map/ppermute | solution.py:513
  46.2 4.4 %collective-permute-start.14 = (f32[40,128]{1,0:T(8,128)S(1)}, f32[40,128]{1,0:T(8,128)S(1)}, u32[]{:S(2)}, u32[]{:S(2)}) collective-permute-start(f32[40,128]{1,0:T(8,128)S(1)} %add_add_fusion.1), channel_id=1, source_target_pairs={{0,96},{32,64},{64,32},{96,0},{128,224},{160,192},{192,160},{224,1... | collective-permute-start | bytes 61448 | tf_op jit(solution)/shard_map/ppermute | solution.py:513
  48.8 2.6 %collective-permute-start.13 = (f32[40,128]{1,0:T(8,128)S(1)}, f32[40,128]{1,0:T(8,128)S(1)}, u32[]{:S(2)}, u32[]{:S(2)}) collective-permute-start(f32[40,128]{1,0:T(8,128)S(1)} %add_add_fusion.1), channel_id=1, source_target_pairs={{0,32},{32,0},{64,96},{96,64},{128,160},{160,128},{192,224},{224,1... | collective-permute-start | bytes 61448 | tf_op jit(solution)/shard_map/ppermute | solution.py:513
  51.5 3.9 %collective-permute-start.16 = (f32[40,128]{1,0:T(8,128)S(1)}, f32[40,128]{1,0:T(8,128)S(1)}, u32[]{:S(2)}, u32[]{:S(2)}) collective-permute-start(f32[40,128]{1,0:T(8,128)S(1)} %add_add_fusion), channel_id=1, source_target_pairs={{0,224},{32,192},{64,160},{96,128},{128,96},{160,64},{192,32},{224... | collective-permute-start | bytes 61448 | tf_op jit(solution)/shard_map/ppermute | solution.py:513
  55.4 6.6 %collective-permute-start.17 = (f32[40,128]{1,0:T(8,128)S(1)}, f32[40,128]{1,0:T(8,128)S(1)}, u32[]{:S(2)}, u32[]{:S(2)}) collective-permute-start(f32[40,128]{1,0:T(8,128)S(1)} %add.43.refs_0_), channel_id=1, source_target_pairs={{0,1},{1,0},{2,3},{3,2},{4,5},{5,4},{6,7},{7,6},{8,9},{9,8},{10,11... | collective-permute-start | bytes 61448 | tf_op jit(solution)/shard_map/ppermute | solution.py:538

commit v5 on v4

--- a/solution.py
+++ b/solution.py
@@ -49,18 +49,20 @@
 def message_kernel(u, kap, dec, index, uall, west, east, row_a, row_b, col_a, col_b, fi, sems, scalars, index_sem):
     index_copy = pltpu.make_async_copy(index, scalars, index_sem)
     index_copy.start()
+    copies = [
+        (
+            pltpu.make_async_copy(u.at[:, x, :], uall.at[x, 0:S, :], sems.at[0, x]),
+            pltpu.make_async_copy(kap.at[:, x, :], uall.at[x, KAP : KAP + FIELDS, :], sems.at[1, x]),
+            pltpu.make_async_copy(dec.at[x : x + 1, :], uall.at[x, DEC : DEC + 1, :], sems.at[2, x]),
+        )
+        for x in range(ROWS)
+    ]
+    for copy, _, _ in copies:
+        copy.start()
     for x in range(ROWS):
         uall[x, S:EXT, :] = jnp.zeros((8, COLS), F32)
-    copies = []
-    for x in range(ROWS):
-        copies.append(
-            (
-                pltpu.make_async_copy(u.at[:, x, :], uall.at[x, 0:S, :], sems.at[0, x]),
-                pltpu.make_async_copy(kap.at[:, x, :], uall.at[x, KAP : KAP + FIELDS, :], sems.at[1, x]),
-                pltpu.make_async_copy(dec.at[x : x + 1, :], uall.at[x, DEC : DEC + 1, :], sems.at[2, x]),
-            )
-        )
-        for copy in copies[x]:
+    for _, *small in copies:
+        for copy in small:
             copy.start()
     index_copy.wait()
     sub = lax.broadcasted_iota(jnp.int32, (8, 128), 0)

time: 73.6 us -> 74.7 us (1.015)
  Pallas kernels: 22.2 us -> 23.4 us
    pallas_call x1, Pallas kernels: 3.23 us -> 4.39 us  [messages(): pl.pallas_call(message_kernel, name='messages', in_specs=[HBM] * 4, out_s...]
where the time goes in v5:
time: 74.7 us; the launch traced here: 74.6 us
  starting transfers between devices  35.3 us (47%)
  Pallas kernels  23.4 us (31%)
  waiting for transfers between devices  14.9 us (20%)
  between operations  0.91 us (1%)
    ppermute x10, starting transfers between devices, swap_sum(): lax.ppermute(value, axis, [(i, i ^ k) for i in range(count)])  18.5 us
    pallas_call x1, Pallas kernels, make_basis(): pl.pallas_call(kernel, name='basis', in_specs=[VM] * 10, out_specs=[HBM,...  11.3 us
    ppermute x10, waiting for transfers between devices, swap_sum(): lax.ppermute(value, axis, [(i, i ^ k) for i in range(count)])  10.2 us
    ppermute x1, starting transfers between devices, shards(): other = lax.ppermute(mine, 'core', swap)  5.71 us
    pallas_call x1, Pallas kernels, interior(): pl.pallas_call(interior_kernel, name='interior', in_specs=[VM] * 6, out_s...  5.37 us
    pallas_call x1, Pallas kernels, messages(): pl.pallas_call(message_kernel, name='messages', in_specs=[HBM] * 4, out_s...  4.39 us
    ppermute x1, starting transfers between devices, shards(): corner_a = lax.ppermute(corner_a, ROWAXIS, pairs(ROWAXIS, 0))  3.44 us
    ppermute x1, starting transfers between devices, shards(): lax.ppermute(col_b, COLAXIS, pairs(COLAXIS, 1))  2.83 us
  transfers between devices with their start and end apart: 18, of which 10 were waited for; matrix products, arithmetic and copies ran while one was open for 0% of the time, Pallas kernels for 7%

profile of v5, /device:TPU:1, one launch (start us, length us, event | category | flops | bytes accessed | tf_op | source)
XLA Modules:
  0.0 74.6 jit_solution(15882787720429416208)
XLA Ops:
  0.6 4.4 %messages.1 = (f32[16,72,1024]{2,1,0:T(8,128)S(1)}, f32[72,128]{1,0:T(8,128)S(1)}, f32[72,128]{1,0:T(8,128)S(1)}, f32[64,2176]{1,0:T(8,128)S(1)}, f32[64,2176]{1...) custom-call(f32[64,16,1024]{2,1,0:T(8,128)} %u.1, f32[4,16,1024]{2,1,0:T(8,128)} %kap.1, ...), custom_call_target="tpu_custom_call" | custom-call | tf_op jit(solution)/shard_map/messages/pallas_call | solution.py:104
  5.0 2.1 %collective-permute-start.2 = (f32[64,2176]{1,0:T(8,128)S(1)}, f32[64,2176]{1,0:T(8,128)S(1)}, u32[]{:S(2)}, u32[]{:S(2)}) collective-permute-start(f32[64,2176]{1,0:T(8,128)S(1)} %get-tuple-element.36), channel_id=1, source_target_pairs={{0,8},{16,24},{32,40},{48,56},{64,72},{80,88},{96,104},{112,120},{... | collective-permute-start | bytes 1671176 | tf_op jit(solution)/shard_map/ppermute | solution.py:527
  7.2 0.7 collective-permute-start.3
  7.8 1.3 %collective-permute-start = (f32[72,128]{1,0:T(8,128)S(1)}, f32[72,128]{1,0:T(8,128)S(1)}, u32[]{:S(2)}, u32[]{:S(2)}) collective-permute-start(f32[72,128]{1,0:T(8,128)S(1)} %get-tuple-element.30), channel_id=1, source_target_pairs={{0,1},{2,3},{4,5},{6,7},{1,0},{3,2},{5,4},{7,6},{8,9},{10,11},{12,... | collective-permute-start | bytes 110600 | tf_op jit(solution)/shard_map/ppermute | solution.py:528
  9.2 2.8 %collective-permute-start.1 = (f32[72,128]{1,0:T(8,128)S(1)}, f32[72,128]{1,0:T(8,128)S(1)}, u32[]{:S(2)}, u32[]{:S(2)}) collective-permute-start(f32[72,128]{1,0:T(8,128)S(1)} %get-tuple-element.31), channel_id=1, source_target_pairs={{1,2},{3,4},{5,6},{2,1},{4,3},{6,5},{9,10},{11,12},{13,14},{10,9},... | collective-permute-start | bytes 110600 | tf_op jit(solution)/shard_map/ppermute | solution.py:528
  12.0 0.0 collective-permute-done.first_from
  12.0 2.7 %collective-permute-done.1.second_from = f32[72,128]{1,0:T(8,128)S(1)} collective-permute-done((f32[72,128]{1,0:T(8,128)S(1)}, f32[72,128]{1,0:T(8,128)S(1)}, u32[]{:S(2)}, u32[]{:S(2)}) %collective-permute-start.1) | collective-permute-done | bytes 36896 | tf_op jit(solution)/shard_map/ppermute | solution.py:528
  14.7 0.1 corners.1
  14.8 3.4 %collective-permute-start.4 = (f32[64,128]{1,0:T(8,128)S(1)}, f32[64,128]{1,0:T(8,128)S(1)}, u32[]{:S(2)}, u32[]{:S(2)}) collective-permute-start(f32[64,128]{1,0:T(8,128)S(1)} %get-tuple-element.38), channel_id=1, source_target_pairs={{0,8},{16,24},{32,40},{48,56},{64,72},{80,88},{96,104},{112,120},{... | collective-permute-start | bytes 98312 | tf_op jit(solution)/shard_map/ppermute | solution.py:530
  18.3 0.7 collective-permute-start.5
  18.9 5.4 %interior.1 = (f32[16,64,1024]{2,1,0:T(8,128)S(1)}, bf16[4,128,1024]{2,1,0:T(8,128)(2,1)S(1)}, bf16[4,128,1024]{2,1,0:T(8,128)(2,1)S(1)}, bf16[4,128,1024]{2,1,0...) custom-call(s32[64,128]{1,0:T(8,128)S(1)} %get-tuple-element.26.fi, ...), custom_call_target="tpu_custom_call" | custom-call | flops 805306368 | bytes 33554432 | tf_op jit(solution)/shard_map/interior/pallas_call | solution.py:277
  24.3 0.0 collective-permute-done.4.nc
  24.3 0.0 collective-permute-done.5.sc
  24.3 0.0 collective-permute-done.2.n1
  24.3 0.0 collective-permute-done.3.s1
  24.3 2.3 %edges.1 = (bf16[4,128,1024]{2,1,0:T(8,128)(2,1)S(1)}, bf16[4,128,1024]{2,1,0:T(8,128)(2,1)S(1)}, f32[40,128]{1,0:T(8,128)S(1)}, f32[40,128]{1,0:T(8,128)S(1)}) custom-call(s32[64,128]{1,0:T(8,128)S(1)} %get-tuple-element.26.fi, f32[16,72,1024]{2,1,0:T(8,128)S(1)} %get-tuple-element.27.uall, f32[72,128]{1,0:T(8,128)S(1)} %get-tuple-element.28.own_w, ...), custom_call_target="tpu_custom_call" | custom-call | tf_op jit(solution)/shard_map/edges/pallas_call | solution.py:380
  26.6 0.1 collective-permute-start.6
  26.7 1.2 %collective-permute-done.6 = f32[40,128]{1,0:T(8,128)S(1)} collective-permute-done((f32[40,128]{1,0:T(8,128)S(1)}, f32[40,128]{1,0:T(8,128)S(1)}, u32[]{:S(2)}, u32[]{:S(2)}) %collective-permute-start.6) | collective-permute-done | bytes 20512 | tf_op jit(solution)/shard_map/ppermute | solution.py:537
  27.9 4.3 %collective-permute-start.9 = (f32[40,128]{1,0:T(8,128)S(1)}, f32[40,128]{1,0:T(8,128)S(1)}, u32[]{:S(2)}, u32[]{:S(2)}) collective-permute-start(f32[40,128]{1,0:T(8,128)S(1)} %add.33), channel_id=1, source_target_pairs={{0,16},{8,24},{16,0},{24,8},{1,17},{9,25},{17,1},{25,9},{2,18},{10... | collective-permute-start | bytes 61448 | tf_op jit(solution)/shard_map/ppermute | solution.py:515
  32.2 2.1 %collective-permute-start.8 = (f32[40,128]{1,0:T(8,128)S(1)}, f32[40,128]{1,0:T(8,128)S(1)}, u32[]{:S(2)}, u32[]{:S(2)}) collective-permute-start(f32[40,128]{1,0:T(8,128)S(1)} %add.33), channel_id=1, source_target_pairs={{0,24},{8,16},{16,8},{24,0},{1,25},{9,17},{17,9},{25,1},{2,26},{10... | collective-permute-start | bytes 61448 | tf_op jit(solution)/shard_map/ppermute | solution.py:515
  34.3 0.0 collective-permute-start.7
  34.3 0.0 collective-permute-done.9
  34.3 1.8 %collective-permute-done.8 = f32[40,128]{1,0:T(8,128)S(1)} collective-permute-done((f32[40,128]{1,0:T(8,128)S(1)}, f32[40,128]{1,0:T(8,128)S(1)}, u32[]{:S(2)}, u32[]{:S(2)}) %collective-permute-start.8) | collective-permute-done | bytes 20512 | tf_op jit(solution)/shard_map/ppermute | solution.py:515
  36.1 1.1 %collective-permute-done.7 = f32[40,128]{1,0:T(8,128)S(1)} collective-permute-done((f32[40,128]{1,0:T(8,128)S(1)}, f32[40,128]{1,0:T(8,128)S(1)}, u32[]{:S(2)}, u32[]{:S(2)}) %collective-permute-start.7) | collective-permute-done | bytes 20512 | tf_op jit(solution)/shard_map/ppermute | solution.py:515
  37.2 3.0 %collective-permute-start.12 = (f32[40,128]{1,0:T(8,128)S(1)}, f32[40,128]{1,0:T(8,128)S(1)}, u32[]{:S(2)}, u32[]{:S(2)}) collective-permute-start(f32[40,128]{1,0:T(8,128)S(1)} %add_add_fusion.2), channel_id=1, source_target_pairs={{0,4},{2,6},{4,0},{6,2},{1,5},{3,7},{5,1},{7,3},{8,12},{10,14},{12... | collective-permute-start | bytes 61448 | tf_op jit(solution)/shard_map/ppermute | solution.py:515
  40.2 0.8 %collective-permute-start.11 = (f32[40,128]{1,0:T(8,128)S(1)}, f32[40,128]{1,0:T(8,128)S(1)}, u32[]{:S(2)}, u32[]{:S(2)}) collective-permute-start(f32[40,128]{1,0:T(8,128)S(1)} %add_add_fusion.2), channel_id=1, source_target_pairs={{0,6},{2,4},{4,2},{6,0},{1,7},{3,5},{5,3},{7,1},{8,14},{10,12},{12... | collective-permute-start | bytes 61448 | tf_op jit(solution)/shard_map/ppermute | solution.py:515
  41.0 0.0 collective-permute-start.10
  41.0 0.4 collective-permute-done.12
  41.4 2.6 %collective-permute-done.11 = f32[40,128]{1,0:T(8,128)S(1)} collective-permute-done((f32[40,128]{1,0:T(8,128)S(1)}, f32[40,128]{1,0:T(8,128)S(1)}, u32[]{:S(2)}, u32[]{:S(2)}) %collective-permute-start.11) | collective-permute-done | bytes 20512 | tf_op jit(solution)/shard_map/ppermute | solution.py:515
  44.1 0.0 collective-permute-done.10
  44.1 3.3 %collective-permute-start.15 = (f32[40,128]{1,0:T(8,128)S(1)}, f32[40,128]{1,0:T(8,128)S(1)}, u32[]{:S(2)}, u32[]{:S(2)}) collective-permute-start(f32[40,128]{1,0:T(8,128)S(1)} %add_add_fusion.1), channel_id=1, source_target_pairs={{0,64},{32,96},{64,0},{96,32},{128,192},{160,224},{192,128},{224,1... | collective-permute-start | bytes 61448 | tf_op jit(solution)/shard_map/ppermute | solution.py:515
  47.3 2.7 %collective-permute-start.14 = (f32[40,128]{1,0:T(8,128)S(1)}, f32[40,128]{1,0:T(8,128)S(1)}, u32[]{:S(2)}, u32[]{:S(2)}) collective-permute-start(f32[40,128]{1,0:T(8,128)S(1)} %add_add_fusion.1), channel_id=1, source_target_pairs={{0,96},{32,64},{64,32},{96,0},{128,224},{160,192},{192,160},{224,1... | collective-permute-start | bytes 61448 | tf_op jit(solution)/shard_map/ppermute | solution.py:515
  50.0 0.2 collective-permute-start.13
  50.2 0.0 collective-permute-done.15
  50.2 1.6 %collective-permute-done.14 = f32[40,128]{1,0:T(8,128)S(1)} collective-permute-done((f32[40,128]{1,0:T(8,128)S(1)}, f32[40,128]{1,0:T(8,128)S(1)}, u32[]{:S(2)}, u32[]{:S(2)}) %collective-permute-start.14) | collective-permute-done | bytes 20512 | tf_op jit(solution)/shard_map/ppermute | solution.py:515
  51.8 0.8 %collective-permute-done.13 = f32[40,128]{1,0:T(8,128)S(1)} collective-permute-done((f32[40,128]{1,0:T(8,128)S(1)}, f32[40,128]{1,0:T(8,128)S(1)}, u32[]{:S(2)}, u32[]{:S(2)}) %collective-permute-start.13) | collective-permute-done | bytes 20512 | tf_op jit(solution)/shard_map/ppermute | solution.py:515
  52.6 2.2 %collective-permute-start.16 = (f32[40,128]{1,0:T(8,128)S(1)}, f32[40,128]{1,0:T(8,128)S(1)}, u32[]{:S(2)}, u32[]{:S(2)}) collective-permute-start(f32[40,128]{1,0:T(8,128)S(1)} %add_add_fusion), channel_id=1, source_target_pairs={{0,224},{32,192},{64,160},{96,128},{128,96},{160,64},{192,32},{224... | collective-permute-start | bytes 61448 | tf_op jit(solution)/shard_map/ppermute | solution.py:515
  54.8 1.7 %collective-permute-done.16 = f32[40,128]{1,0:T(8,128)S(1)} collective-permute-done((f32[40,128]{1,0:T(8,128)S(1)}, f32[40,128]{1,0:T(8,128)S(1)}, u32[]{:S(2)}, u32[]{:S(2)}) %collective-permute-start.16) | collective-permute-done | bytes 20512 | tf_op jit(solution)/shard_map/ppermute | solution.py:515
  56.6 5.7 %collective-permute-start.17 = (f32[40,128]{1,0:T(8,128)S(1)}, f32[40,128]{1,0:T(8,128)S(1)}, u32[]{:S(2)}, u32[]{:S(2)}) collective-permute-start(f32[40,128]{1,0:T(8,128)S(1)} %add.43.refs_0_), channel_id=1, source_target_pairs={{0,1},{1,0},{2,3},{3,2},{4,5},{5,4},{6,7},{7,6},{8,9},{9,8},{10,11... | collective-permute-start | bytes 61448 | tf_op jit(solution)/shard_map/ppermute | solution.py:540
  62.3 0.8 %collective-permute-done.17.refs_1_ = f32[40,128]{1,0:T(8,128)S(1)} collective-permute-done((f32[40,128]{1,0:T(8,128)S(1)}, f32[40,128]{1,0:T(8,128)S(1)}, u32[]{:S(2)}, u32[]{:S(2)}) %collective-permute-start.17) | collective-permute-done | bytes 20512 | tf_op jit(solution)/shard_map/ppermute | solution.py:540
  63.1 11.3 %basis.1 = (f32[128,16,1024]{2,1,0:T(8,128)}, f32[128,128]{1,0:T(8,128)}) custom-call(f32[40,128]{1,0:T(8,128)S(1)} %add.43.refs_0_, f32[40,128]{1,0:T(8,128)S(1)} %collective-permute-done.17.refs_1_, bf16[4,128,1024]{2,1,0:T(8,128)(2,1)S(1)} %get-tuple-element.42.refs_2_, bf16[4,128,1024]{2,1,0:T(8,128)(2,1)S(1)} %get-tuple-element.43.refs_3_, ...), custom_call_target="tpu_custom_call" | custom-call | tf_op jit(solution)/shard_map/basis/pallas_call | solution.py:485
  (5 shorter events, 0.0 us)
Async XLA Ops:
  5.0 19.3 %collective-permute-start.2 = (f32[64,2176]{1,0:T(8,128)S(1)}, f32[64,2176]{1,0:T(8,128)S(1)}, u32[]{:S(2)}, u32[]{:S(2)}) collective-permute-start(f32[64,2176]{1,0:T(8,128)S(1)} %get-tuple-element.36), channel_id=1, source_target_pairs={{0,8},{16,24},{32,40},{48,56},{64,72},{80,88},{96,104},{112,120},{... | collective-permute-start | bytes 1671176 | tf_op jit(solution)/shard_map/ppermute | solution.py:527
  7.2 17.2 %collective-permute-start.3 = (f32[64,2176]{1,0:T(8,128)S(1)}, f32[64,2176]{1,0:T(8,128)S(1)}, u32[]{:S(2)}, u32[]{:S(2)}) collective-permute-start(f32[64,2176]{1,0:T(8,128)S(1)} %get-tuple-element.37), channel_id=1, source_target_pairs={{8,16},{24,32},{40,48},{56,64},{72,80},{88,96},{104,112},{120,128}... | collective-permute-start | bytes 1671176 | tf_op jit(solution)/shard_map/ppermute | solution.py:527
  7.8 4.2 %collective-permute-start = (f32[72,128]{1,0:T(8,128)S(1)}, f32[72,128]{1,0:T(8,128)S(1)}, u32[]{:S(2)}, u32[]{:S(2)}) collective-permute-start(f32[72,128]{1,0:T(8,128)S(1)} %get-tuple-element.30), channel_id=1, source_target_pairs={{0,1},{2,3},{4,5},{6,7},{1,0},{3,2},{5,4},{7,6},{8,9},{10,11},{12,... | collective-permute-start | bytes 110600 | tf_op jit(solution)/shard_map/ppermute | solution.py:528
  9.2 5.6 %collective-permute-start.1 = (f32[72,128]{1,0:T(8,128)S(1)}, f32[72,128]{1,0:T(8,128)S(1)}, u32[]{:S(2)}, u32[]{:S(2)}) collective-permute-start(f32[72,128]{1,0:T(8,128)S(1)} %get-tuple-element.31), channel_id=1, source_target_pairs={{1,2},{3,4},{5,6},{2,1},{4,3},{6,5},{9,10},{11,12},{13,14},{10,9},... | collective-permute-start | bytes 110600 | tf_op jit(solution)/shard_map/ppermute | solution.py:528
  14.8 9.5 %collective-permute-start.4 = (f32[64,128]{1,0:T(8,128)S(1)}, f32[64,128]{1,0:T(8,128)S(1)}, u32[]{:S(2)}, u32[]{:S(2)}) collective-permute-start(f32[64,128]{1,0:T(8,128)S(1)} %get-tuple-element.38), channel_id=1, source_target_pairs={{0,8},{16,24},{32,40},{48,56},{64,72},{80,88},{96,104},{112,120},{... | collective-permute-start | bytes 98312 | tf_op jit(solution)/shard_map/ppermute | solution.py:530
  18.3 6.0 %collective-permute-start.5 = (f32[64,128]{1,0:T(8,128)S(1)}, f32[64,128]{1,0:T(8,128)S(1)}, u32[]{:S(2)}, u32[]{:S(2)}) collective-permute-start(f32[64,128]{1,0:T(8,128)S(1)} %get-tuple-element.39), channel_id=1, source_target_pairs={{8,16},{24,32},{40,48},{56,64},{72,80},{88,96},{104,112},{120,128}... | collective-permute-start | bytes 98312 | tf_op jit(solution)/shard_map/ppermute | solution.py:531
  26.6 1.3 %collective-permute-start.6 = (f32[40,128]{1,0:T(8,128)S(1)}, f32[40,128]{1,0:T(8,128)S(1)}, u32[]{:S(2)}, u32[]{:S(2)}) collective-permute-start(f32[40,128]{1,0:T(8,128)S(1)} %get-tuple-element.41), channel_id=1, source_target_pairs={{0,1},{1,0},{2,3},{3,2},{4,5},{5,4},{6,7},{7,6},{8,9},{9,8},{10,11... | collective-permute-start | bytes 61448 | tf_op jit(solution)/shard_map/ppermute | solution.py:537
  27.9 6.4 %collective-permute-start.9 = (f32[40,128]{1,0:T(8,128)S(1)}, f32[40,128]{1,0:T(8,128)S(1)}, u32[]{:S(2)}, u32[]{:S(2)}) collective-permute-start(f32[40,128]{1,0:T(8,128)S(1)} %add.33), channel_id=1, source_target_pairs={{0,16},{8,24},{16,0},{24,8},{1,17},{9,25},{17,1},{25,9},{2,18},{10... | collective-permute-start | bytes 61448 | tf_op jit(solution)/shard_map/ppermute | solution.py:515
  32.2 3.8 %collective-permute-start.8 = (f32[40,128]{1,0:T(8,128)S(1)}, f32[40,128]{1,0:T(8,128)S(1)}, u32[]{:S(2)}, u32[]{:S(2)}) collective-permute-start(f32[40,128]{1,0:T(8,128)S(1)} %add.33), channel_id=1, source_target_pairs={{0,24},{8,16},{16,8},{24,0},{1,25},{9,17},{17,9},{25,1},{2,26},{10... | collective-permute-start | bytes 61448 | tf_op jit(solution)/shard_map/ppermute | solution.py:515
  34.3 2.9 %collective-permute-start.7 = (f32[40,128]{1,0:T(8,128)S(1)}, f32[40,128]{1,0:T(8,128)S(1)}, u32[]{:S(2)}, u32[]{:S(2)}) collective-permute-start(f32[40,128]{1,0:T(8,128)S(1)} %add.33), channel_id=1, source_target_pairs={{0,8},{8,0},{16,24},{24,16},{1,9},{9,1},{17,25},{25,17},{2,10},{10... | collective-permute-start | bytes 61448 | tf_op jit(solution)/shard_map/ppermute | solution.py:515
  37.2 4.2 %collective-permute-start.12 = (f32[40,128]{1,0:T(8,128)S(1)}, f32[40,128]{1,0:T(8,128)S(1)}, u32[]{:S(2)}, u32[]{:S(2)}) collective-permute-start(f32[40,128]{1,0:T(8,128)S(1)} %add_add_fusion.2), channel_id=1, source_target_pairs={{0,4},{2,6},{4,0},{6,2},{1,5},{3,7},{5,1},{7,3},{8,12},{10,14},{12... | collective-permute-start | bytes 61448 | tf_op jit(solution)/shard_map/ppermute | solution.py:515
  40.2 3.8 %collective-permute-start.11 = (f32[40,128]{1,0:T(8,128)S(1)}, f32[40,128]{1,0:T(8,128)S(1)}, u32[]{:S(2)}, u32[]{:S(2)}) collective-permute-start(f32[40,128]{1,0:T(8,128)S(1)} %add_add_fusion.2), channel_id=1, source_target_pairs={{0,6},{2,4},{4,2},{6,0},{1,7},{3,5},{5,3},{7,1},{8,14},{10,12},{12... | collective-permute-start | bytes 61448 | tf_op jit(solution)/shard_map/ppermute | solution.py:515
  41.0 3.1 %collective-permute-start.10 = (f32[40,128]{1,0:T(8,128)S(1)}, f32[40,128]{1,0:T(8,128)S(1)}, u32[]{:S(2)}, u32[]{:S(2)}) collective-permute-start(f32[40,128]{1,0:T(8,128)S(1)} %add_add_fusion.2), channel_id=1, source_target_pairs={{0,2},{2,0},{4,6},{6,4},{1,3},{3,1},{5,7},{7,5},{8,10},{10,8},{12,... | collective-permute-start | bytes 61448 | tf_op jit(solution)/shard_map/ppermute | solution.py:515
  44.1 6.1 %collective-permute-start.15 = (f32[40,128]{1,0:T(8,128)S(1)}, f32[40,128]{1,0:T(8,128)S(1)}, u32[]{:S(2)}, u32[]{:S(2)}) collective-permute-start(f32[40,128]{1,0:T(8,128)S(1)} %add_add_fusion.1), channel_id=1, source_target_pairs={{0,64},{32,96},{64,0},{96,32},{128,192},{160,224},{192,128},{224,1... | collective-permute-start | bytes 61448 | tf_op jit(solution)/shard_map/ppermute | solution.py:515
  47.3 4.4 %collective-permute-start.14 = (f32[40,128]{1,0:T(8,128)S(1)}, f32[40,128]{1,0:T(8,128)S(1)}, u32[]{:S(2)}, u32[]{:S(2)}) collective-permute-start(f32[40,128]{1,0:T(8,128)S(1)} %add_add_fusion.1), channel_id=1, source_target_pairs={{0,96},{32,64},{64,32},{96,0},{128,224},{160,192},{192,160},{224,1... | collective-permute-start | bytes 61448 | tf_op jit(solution)/shard_map/ppermute | solution.py:515
  50.0 2.6 %collective-permute-start.13 = (f32[40,128]{1,0:T(8,128)S(1)}, f32[40,128]{1,0:T(8,128)S(1)}, u32[]{:S(2)}, u32[]{:S(2)}) collective-permute-start(f32[40,128]{1,0:T(8,128)S(1)} %add_add_fusion.1), channel_id=1, source_target_pairs={{0,32},{32,0},{64,96},{96,64},{128,160},{160,128},{192,224},{224,1... | collective-permute-start | bytes 61448 | tf_op jit(solution)/shard_map/ppermute | solution.py:515
  52.6 3.9 %collective-permute-start.16 = (f32[40,128]{1,0:T(8,128)S(1)}, f32[40,128]{1,0:T(8,128)S(1)}, u32[]{:S(2)}, u32[]{:S(2)}) collective-permute-start(f32[40,128]{1,0:T(8,128)S(1)} %add_add_fusion), channel_id=1, source_target_pairs={{0,224},{32,192},{64,160},{96,128},{128,96},{160,64},{192,32},{224... | collective-permute-start | bytes 61448 | tf_op jit(solution)/shard_map/ppermute | solution.py:515
  56.6 6.6 %collective-permute-start.17 = (f32[40,128]{1,0:T(8,128)S(1)}, f32[40,128]{1,0:T(8,128)S(1)}, u32[]{:S(2)}, u32[]{:S(2)}) collective-permute-start(f32[40,128]{1,0:T(8,128)S(1)} %add.43.refs_0_), channel_id=1, source_target_pairs={{0,1},{1,0},{2,3},{3,2},{4,5},{5,4},{6,7},{7,6},{8,9},{9,8},{10,11... | collective-permute-start | bytes 61448 | tf_op jit(solution)/shard_map/ppermute | solution.py:540
